TPU v7x, 768 devices: a whole 4x8x12 slice. The times are simulated.
768 devices in a mesh: grp: 32 (over x, y), rep: 24 (over z, core).
Axes of the slice: x: 4, y: 8, z: 12, core: 2. Of those that a mesh axis runs over, the one named last changes fastest.
Arguments:
- pooled_grad: bfloat16 [786432, 256], P(('grp', 'rep')), may hold values from -6 to 6
- lookup_bag: int32 [768, 2048], P(('grp', 'rep')), may hold values from 0 to 1023, never falling along the last dimension, each value on 1 to 8 neighbouring positions
- saved_quotient: bfloat16 [1572864, 256], P(('grp', 'rep')), may hold values from -6 to 6
- saved_remainder: bfloat16 [1572864, 256], P(('grp', 'rep')), may hold values from -6 to 6
- quotient_slot: int32 [768, 2048], P(('grp', 'rep')), may hold values from 0 to 1535
- quotient_rows: int32 [768, 1536], P(('grp', 'rep')), may hold values from 0 to 255
- remainder_slot: int32 [768, 2048], P(('grp', 'rep')), may hold values from 0 to 511
- remainder_rows: int32 [768, 512], P(('grp', 'rep')), may hold values from 0 to 63
- tower_inputs: bfloat16 [98304, 512], P(('grp', 'rep')), may hold values from -6 to 6
- tower_cotangent: bfloat16 [98304, 256], P(('grp', 'rep')), may hold values from -0.01953125 to 0.01953125
Outputs:
- quotient_grad: float32 [196608, 256], P(('grp', 'rep'))
- remainder_grad: float32 [2048, 256], P('grp')
- tower_grad: float32 [512, 256], replicated
Inputs may be any that keep to these rules, and one draw needn't show every extreme that they name: `lookup_bag`: along each device's row the bag number never falls and each of the 1024 bags holds 1 to 8 lookups. `quotient_slot`: slot s belongs to the owner device with number s // 2. `remainder_slot`: slot s belongs to the owners with grp index s // 16.
All inputs are finite; a program needn't handle non-finite values.
Results may differ from a plain program's by a relative error of at most 0.0003.
Values sent between devices are 32-bit elements; how exact they have to be, the bound alone decides.
No kernel may reach another device: no remote copies, remote signals or barrier semaphores. Data moves between devices by JAX's collectives and lax.ppermute only.
A program may use at most 32 MiB of HBM per device.

v0:
```python
import jax
import jax.numpy as jnp
from jax import lax
from jax.sharding import PartitionSpec as P

QROWS_DEV = 256
RROWS_DEV = 64


def local(
    pooled_grad,
    lookup_bag,
    saved_quotient,
    saved_remainder,
    quotient_slot,
    quotient_rows,
    remainder_slot,
    remainder_rows,
    tower_inputs,
    tower_cotangent,
):
    groups = lax.axis_size("grp")
    replicas = lax.axis_size("rep")
    columns = pooled_grad.shape[1]
    quotient_count = quotient_rows.shape[1]
    remainder_count = remainder_rows.shape[1]
    tower_part = lax.dot_general(
        tower_inputs, tower_cotangent, (((0,), (0,)), ((), ())), preferred_element_type=jnp.float32
    )
    tower_grad = lax.psum(tower_part, ("grp", "rep"))
    gathered = jnp.take(pooled_grad, lookup_bag[0], axis=0).astype(jnp.float32)
    quotient_terms = gathered * saved_remainder.astype(jnp.float32)
    remainder_terms = gathered * saved_quotient.astype(jnp.float32)
    quotient_sums = jax.ops.segment_sum(
        quotient_terms, quotient_slot[0], num_segments=quotient_count
    )
    remainder_sums = jax.ops.segment_sum(
        remainder_terms, remainder_slot[0], num_segments=remainder_count
    )
    quotient_cap = quotient_count // (groups * replicas)
    outgoing = quotient_sums.reshape(groups, replicas, quotient_cap, columns)
    row_labels = quotient_rows[0].reshape(groups, replicas, quotient_cap).astype(jnp.float32)
    arrived, arrived_rows = (
        lax.all_to_all(
            lax.all_to_all(outgoing, "grp", split_axis=0, concat_axis=0, tiled=True),
            "rep",
            split_axis=1,
            concat_axis=1,
            tiled=True,
        ),
        lax.all_to_all(
            lax.all_to_all(row_labels, "grp", split_axis=0, concat_axis=0, tiled=True),
            "rep",
            split_axis=1,
            concat_axis=1,
            tiled=True,
        ),
    )
    quotient_grad = jax.ops.segment_sum(
        arrived.reshape(-1, columns),
        arrived_rows.reshape(-1).astype(jnp.int32),
        num_segments=QROWS_DEV,
    )
    remainder_cap = remainder_count // groups
    target = (
        jnp.arange(remainder_count, dtype=jnp.int32) // remainder_cap * RROWS_DEV
        + remainder_rows[0]
    )
    row_count = lax.axis_size("grp") * RROWS_DEV
    inside = (target >= 0) & (target < row_count)
    labels = jnp.where(inside, target, row_count)
    remainder_local = lax.psum_scatter(
        jax.ops.segment_sum(remainder_sums, labels, num_segments=row_count + 1)[:row_count],
        "grp",
        scatter_dimension=0,
        tiled=True,
    )
    remainder_grad = lax.psum(remainder_local, "rep")
    return (quotient_grad, remainder_grad, tower_grad)


def solution(mesh):
    in_specs = (
        P(("grp", "rep"), None),
        P(("grp", "rep"), None),
        P(("grp", "rep"), None),
        P(("grp", "rep"), None),
        P(("grp", "rep"), None),
        P(("grp", "rep"), None),
        P(("grp", "rep"), None),
        P(("grp", "rep"), None),
        P(("grp", "rep"), None),
        P(("grp", "rep"), None),
    )
    out_specs = (P(("grp", "rep"), None), P("grp", None), P())
    return jax.shard_map(local, mesh=mesh, in_specs=in_specs, out_specs=out_specs, check_vma=False)
```

profile of v0, /device:TPU:2, one launch (start us, length us, event | category | flops | bytes accessed | tf_op | source)
XLA Modules:
  0.0 747.5 jit_solution(9573428220583297221)
XLA Ops:
  8.0 0.0 copy-start
  8.0 0.8 convert_reduce_fusion
  8.8 0.3 convert_element_type.29
  9.1 0.9 copy.21
  10.0 13.1 %all-to-all-start = ((f32[32,24,2]{1,2,0:T(2,128)}), f32[32,24,2]{1,2,0:T(2,128)S(1)}, u32[]{:S(2)}, u32[]{:S(2)}) async-start(f32[32,24,2]{1,2,0:T(2,128)} %copy.21), calls=%async_computation | async-start | bytes 65536 | tf_op jit(solution)/shard_map/all_to_all | solution.py:52
  23.1 0.7 compare_select_fusion
  23.8 0.7 compare_and_fusion
  24.5 0.0 copy-done
  24.5 7.5 %gather_fusion = bf16[2048,256]{1,0:T(8,128)(2,1)S(1)} fusion(bf16[1024,256]{1,0:T(8,128)(2,1)S(1)} %copy-done, s32[2048]{0:T(1024)S(1)} %broadcast_clamp_fusion), kind=kCustom, calls=%fused_computation | custom fusion | bytes 2105344 | tf_op jit(solution)/shard_map/jit(_take)/gather | solution.py:31
  32.0 13.5 %scatter_custom_fusion = f32[1536,256]{1,0:T(8,128)S(1)} fusion(s32[2048]{0:T(1024)} %bitcast.14, bf16[2048,256]{1,0:T(8,128)(2,1)} %param.13, f32[]{:T(128)} %constant.22.clone.1, bf16[2048,256]{1,0:T(8,128)(2,1)S(1)} %gather_fusion, pred[2048]{0:T(1024)(128)(4,1)S(1)} %compare_and_fusion, bf16[]{:T(256)} %constant.37.clone.1), kind=kCustom, calls=%fused_computation.7 | custom fusion | flops 2621440 | bytes 3673088 | tf_op jit(solution)/shard_map/scatter-add | solution.py:34
  45.6 2.1 reshape.118
  47.7 0.0 copy-start.1
  47.7 0.0 all-to-all-done
  47.7 10.0 %all-to-all-start.2 = ((f32[32,24,2,256]{3,2,1,0:T(2,128)}), f32[32,24,2,256]{3,2,1,0:T(2,128)}, u32[]{:S(2)}, u32[]{:S(2)}) async-start(f32[32,24,2,256]{3,2,1,0:T(2,128)} %reshape.118), calls=%async_computation.2 | async-start | bytes 3145728 | tf_op jit(solution)/shard_map/all_to_all | solution.py:45
  57.7 0.0 copy-start.4
  57.7 0.0 reduce-scatter.2.cloned.1.call-start
  57.8 0.0 copy-done.1
  57.8 13.0 %scatter_custom_fusion.2 = f32[512,256]{1,0:T(8,128)S(1)} fusion(s32[2048]{0:T(1024)} %bitcast.15, bf16[2048,256]{1,0:T(8,128)(2,1)S(1)} %copy-done.1, bf16[2048,256]{1,0:T(8,128)(2,1)S(1)} %gather_fusion, pred[2048]{0:T(1024)(128)(4,1)S(1)} %compare_and_fusion, bf16[]{:T(256)} %constant.37.clone.1, f32[]{:T(128)} %constant.22.clone.1), kind=kCustom, calls=%fused_computation.8 | custom fusion | flops 2621440 | bytes 2624512 | tf_op jit(solution)/shard_map/scatter-add | solution.py:37
  70.8 0.0 copy-done.4
  70.8 4.0 scatter_custom_fusion.3
  74.8 1.5 slice.6
  76.3 0.0 reduce-scatter.2.cloned.1.call-update
  76.3 0.7 copy.22
  77.0 14.7 %all-to-all-done.2 = f32[32,24,2,256]{3,2,1,0:T(2,128)} async-done(((f32[32,24,2,256]{3,2,1,0:T(2,128)}), f32[32,24,2,256]{3,2,1,0:T(2,128)}, u32[]{:S(2)}, u32[]{:S(2)}) %all-to-all-start.2) | async-done | bytes 1572896 | tf_op jit(solution)/shard_map/all_to_all | solution.py:45
  91.7 14.9 %all-to-all-start.1 = ((f32[32,24,2]{0,2,1:T(2,128)}), f32[32,24,2]{0,2,1:T(2,128)S(1)}, u32[]{:S(2)}, u32[]{:S(2)}) async-start(f32[32,24,2]{0,2,1:T(2,128)} %copy.22), calls=%async_computation.1 | async-start | bytes 49152 | tf_op jit(solution)/shard_map/all_to_all | solution.py:51
  106.6 3.5 copy.25
  110.0 0.0 copy-start.2
  110.0 0.0 copy-start.3
  110.0 6.5 all-to-all-done.1
  116.6 4.0 all-to-all-start.3
  120.5 0.0 all-reduce.5.cloned.1.call-start
  120.6 0.0 copy-done.2
  120.6 0.0 copy-done.3
  120.6 1.0 fusion.12
  121.7 0.0 all-reduce.5.cloned.1.call-update
  121.7 0.0 all-reduce.3.cloned.1.call-start
  121.7 183.8 %reduce-scatter.2.cloned.1.call-done = f32[64,256]{1,0:T(8,128)} async-done(((f32[2048,256]{1,0:T(8,128)}), f32[64,256]{1,0:T(8,128)}) %reduce-scatter.2.cloned.1.call-update) | async-done | bytes 65552 | tf_op jit(solution)/shard_map/reduce_scatter | solution.py:72
  305.5 0.0 all-reduce.3.cloned.1.call-update
  305.6 0.2 copy.24
  305.8 0.2 reshape.138
  306.0 0.0 all-to-all-done.3
  306.0 2.0 copy.26
  308.1 2.4 reshape.140
  310.4 9.5 %scatter_custom_fusion.1 = f32[256,256]{1,0:T(8,128)} fusion(s32[1536]{0:T(1024)S(1)} %reshape.138, f32[1536,256]{1,0:T(8,128)S(1)} %reshape.140, f32[]{:T(128)} %constant.22.clone.1), kind=kCustom, calls=%fused_computation.16 | custom fusion | flops 393216 | bytes 262148 | tf_op jit(solution)/shard_map/scatter-add | solution.py:59
  319.9 267.1 %all-reduce.5.cloned.1.call-done = f32[512,256]{1,0:T(8,128)} async-done(((f32[512,256]{1,0:T(8,128)}), f32[512,256]{1,0:T(8,128)}) %all-reduce.5.cloned.1.call-update) | async-done | bytes 524304 | tf_op jit(solution)/shard_map/psum | solution.py:30
  587.0 149.7 %all-reduce.3.cloned.1.call-done = f32[64,256]{1,0:T(8,128)} async-done(((f32[64,256]{1,0:T(8,128)}), f32[64,256]{1,0:T(8,128)}) %all-reduce.3.cloned.1.call-update) | async-done | bytes 65552 | tf_op jit(solution)/shard_map/psum | solution.py:78
  736.7 1.5 copy.30
  738.2 1.9 copy.31
  (3 shorter events, 0.0 us)
Async XLA Ops:
  8.0 16.5 %copy-start = (bf16[1024,256]{1,0:T(8,128)(2,1)S(1)}, bf16[1024,256]{1,0:T(8,128)(2,1)}, u32[]{:S(2)}) copy-start(bf16[1024,256]{1,0:T(8,128)(2,1)} %param.10) | copy-start | bytes 1572868
  10.0 37.7 %all-to-all-start = ((f32[32,24,2]{1,2,0:T(2,128)}), f32[32,24,2]{1,2,0:T(2,128)S(1)}, u32[]{:S(2)}, u32[]{:S(2)}) async-start(f32[32,24,2]{1,2,0:T(2,128)} %copy.21), calls=%async_computation | async-start | bytes 65536 | tf_op jit(solution)/shard_map/all_to_all | solution.py:52
  47.7 10.1 %copy-start.1 = (bf16[2048,256]{1,0:T(8,128)(2,1)S(1)}, bf16[2048,256]{1,0:T(8,128)(2,1)}, u32[]{:S(2)}) copy-start(bf16[2048,256]{1,0:T(8,128)(2,1)} %param.12) | copy-start | bytes 3145732
  47.7 44.0 %all-to-all-start.2 = ((f32[32,24,2,256]{3,2,1,0:T(2,128)}), f32[32,24,2,256]{3,2,1,0:T(2,128)}, u32[]{:S(2)}, u32[]{:S(2)}) async-start(f32[32,24,2,256]{3,2,1,0:T(2,128)} %reshape.118), calls=%async_computation.2 | async-start | bytes 3145728 | tf_op jit(solution)/shard_map/all_to_all | solution.py:45
  57.7 13.1 %copy-start.4 = (s32[1,512]{1,0:T(1,128)S(1)}, s32[1,512]{1,0:T(1,128)}, u32[]{:S(2)}) copy-start(s32[1,512]{1,0:T(1,128)} %param.17) | copy-start | bytes 6148
  57.7 247.8 %reduce-scatter.2.cloned.1.call-start = ((), (), s32[]{:S(2)}) async-start(), calls=%async_computation.5 | async-start | bytes 2162688 | tf_op jit(solution)/shard_map/reduce_scatter | solution.py:72
  91.7 24.9 %all-to-all-start.1 = ((f32[32,24,2]{0,2,1:T(2,128)}), f32[32,24,2]{0,2,1:T(2,128)S(1)}, u32[]{:S(2)}, u32[]{:S(2)}) async-start(f32[32,24,2]{0,2,1:T(2,128)} %copy.22), calls=%async_computation.1 | async-start | bytes 49152 | tf_op jit(solution)/shard_map/all_to_all | solution.py:51
  110.0 10.6 %copy-start.2 = (bf16[128,512]{1,0:T(8,128)(2,1)S(1)}, bf16[128,512]{1,0:T(8,128)(2,1)}, u32[]{:S(2)}) copy-start(bf16[128,512]{1,0:T(8,128)(2,1)} %param.18) | copy-start | bytes 393220
  110.0 10.6 %copy-start.3 = (bf16[128,256]{1,0:T(8,128)(2,1)S(1)}, bf16[128,256]{1,0:T(8,128)(2,1)}, u32[]{:S(2)}) copy-start(bf16[128,256]{1,0:T(8,128)(2,1)} %param.19) | copy-start | bytes 196612
  116.6 189.5 %all-to-all-start.3 = ((f32[32,24,2,256]{3,2,0,1:T(2,128)}), f32[32,24,2,256]{3,2,0,1:T(2,128)S(1)}, u32[]{:S(2)}, u32[]{:S(2)}) async-start(f32[32,24,2,256]{3,2,0,1:T(2,128)} %copy.25), calls=%async_computation.3 | async-start | bytes 3145728 | tf_op jit(solution)/shard_map/all_to_all | solution.py:44
  120.5 466.4 %all-reduce.5.cloned.1.call-start = ((), (), s32[]{:S(2)}) async-start(), calls=%async_computation.7 | async-start | bytes 1048576 | tf_op jit(solution)/shard_map/psum | solution.py:30
  121.7 615.0 %all-reduce.3.cloned.1.call-start = ((), (), s32[]{:S(2)}) async-start(), calls=%async_computation.6 | async-start | bytes 131072 | tf_op jit(solution)/shard_map/psum | solution.py:78
Sparse Core Ops, SparseCore 0:
  76.4 229.0 reduce-scatter.1
Sparse Core Ops, SparseCore 1:
  127.0 460.0 all-reduce.4
  589.2 147.5 all-reduce.2
where the time goes:
time: 748 us; the launch traced here: 747 us
  waiting for transfers between devices  622 us (83%)
  other arithmetic  42.2 us (6%)
  starting transfers between devices  42.2 us (6%)
  local copies, waits for them, and re-layouts  24.7 us (3%)
  between operations  15.7 us (2%)
    psum x1, waiting for transfers between devices, local(): tower_grad = lax.psum(tower_part, ('grp', 'rep'))  267 us
    reduce_scatter x1, waiting for transfers between devices, local(): lax.psum_scatter(jax.ops.segment_sum(remainder_sums, labels, num_segments...  184 us
    psum x1, waiting for transfers between devices, local(): remainder_grad = lax.psum(remainder_local, 'rep')  150 us
  transfers between devices with their start and end apart: 7, of which 5 were waited for; matrix products, arithmetic and copies ran while one was open for 8% of the time, Pallas kernels for 0%

commit v1 on v0

v1 whole, which is shorter than its diff:
```python
import jax
import jax.numpy as jnp
from jax import lax
from jax.experimental import pallas as pl
from jax.experimental.pallas import tpu as pltpu
from jax.sharding import Mesh
from jax.sharding import PartitionSpec as P

E = 256
LANES = 128
LOOK = 2048
BAGS = 1024
QCAP = 2
RCAP = 16
QROWS = 256
RROWS = 64
NX, NY, NZ, NC = 4, 8, 12, 2
GRP = NX * NY
DEVICES = GRP * NZ * NC
HID = 512
TROWS = HID // GRP
PIECE = 72
MESSAGE = 5
F32 = jnp.float32
BF16 = jnp.bfloat16
AXES = ("x", "y", "z", "c")
VMEM = pl.BlockSpec(memory_space=pltpu.VMEM)
SMEM = pl.BlockSpec(memory_space=pltpu.SMEM)


def call(body, out_shape, inputs, specs, scratch=(), flops=0, nbytes=0):
    return pl.pallas_call(
        body,
        out_shape=out_shape,
        in_specs=specs,
        out_specs=jax.tree.map(lambda _: VMEM, out_shape),
        scratch_shapes=list(scratch),
        compiler_params=pltpu.CompilerParams(vmem_limit_bytes=32 * 1024 * 1024),
        cost_estimate=pl.CostEstimate(flops=flops, bytes_accessed=nbytes, transcendentals=0),
    )(*inputs)


def split_terms(bag_smem, bag_ref, pooled_ref, saved_ref, parts_ref):
    lane = lax.broadcasted_iota(jnp.int32, (LANES, LANES), 1)
    for block in range(LOOK // LANES):
        rows = pl.ds(block * LANES, LANES)
        first = jnp.minimum(bag_smem[0, block * LANES] // 16 * 16, BAGS - 2 * LANES)
        first = pl.multiple_of(first, 16)
        row = bag_ref[0:1, block * LANES : (block + 1) * LANES] - first
        column = jnp.transpose(jnp.broadcast_to(row, (LANES, LANES)).astype(F32)).astype(jnp.int32)
        pick = jnp.concatenate([column == lane, column == lane + LANES], axis=1)
        pick = jnp.where(pick, 1.0, 0.0).astype(BF16)
        gathered = jnp.dot(pick, pooled_ref[pl.ds(first, 2 * LANES), :], preferred_element_type=F32)
        terms = gathered * saved_ref[rows, :].astype(F32)
        high = terms.astype(BF16)
        parts_ref[rows, 0:E] = high
        parts_ref[rows, E:] = (terms - high.astype(F32)).astype(BF16)


def one_hot(index_row, first, count, step=1):
    number = lax.broadcasted_iota(jnp.int32, (count, index_row.shape[1]), 0) * step + first
    return jnp.where(number == index_row, 1.0, 0.0).astype(BF16)


def sums(pick, parts):
    both = jnp.dot(pick, parts, preferred_element_type=F32)
    return both[:, :E] + both[:, E:]


def small_kernel(bag_smem, bag_ref, pooled_ref, saved_ref, slot_ref, rows_ref, tin_ref, tcot_ref, out_ref, parts_ref):
    tower = lax.dot_general(tin_ref[...], tcot_ref[...], (((0,), (0,)), ((), ())), preferred_element_type=F32)
    tower = tower.reshape(GRP, TROWS, E)
    out_ref[:, 32:48, :] = tower[:, :, :LANES]
    out_ref[:, 48:64, :] = tower[:, :, LANES:]
    labels = jnp.broadcast_to(rows_ref[...], (GRP, GRP * RCAP))
    slot = lax.broadcasted_iota(jnp.int32, (GRP, GRP * RCAP), 1)
    group = lax.broadcasted_iota(jnp.int32, (GRP, GRP * RCAP), 0)
    labels = jnp.where(slot // RCAP == group, labels, 0).astype(F32).astype(BF16)
    slot = lax.broadcasted_iota(jnp.int32, (GRP * RCAP, LANES), 0)
    lane = lax.broadcasted_iota(jnp.int32, (GRP * RCAP, LANES), 1)
    spread = jnp.where(slot % RCAP == lane % RCAP, 1.0, 0.0).astype(BF16)
    labels = jnp.dot(labels, spread, preferred_element_type=F32)
    out_ref[:, 64:72, :] = jnp.broadcast_to(labels[:, None, :], (GRP, 8, LANES))
    split_terms(bag_smem, bag_ref, pooled_ref, saved_ref, parts_ref)
    slots = slot_ref[...]
    for half in range(2):
        found = sums(one_hot(slots, half * 256, 256), parts_ref[...]).reshape(GRP // 2, RCAP, E)
        groups = pl.ds(half * (GRP // 2), GRP // 2)
        out_ref[groups, 0:16, :] = found[:, :, :LANES]
        out_ref[groups, 16:32, :] = found[:, :, LANES:]


def large_kernel(bag_smem, bag_ref, pooled_ref, saved_ref, slot_ref, label_ref, out_ref, parts_ref):
    split_terms(bag_smem, bag_ref, pooled_ref, saved_ref, parts_ref)
    slots = slot_ref[...]
    chunk = 256
    for block in range(DEVICES // chunk):
        base = block * chunk * MESSAGE
        for p in range(QCAP):
            found = sums(one_hot(slots, block * chunk * QCAP + p, chunk, QCAP), parts_ref[...])
            for h in range(2):
                out_ref[pl.ds(base + 2 * p + h, chunk, stride=MESSAGE), :] = found[:, h * LANES : (h + 1) * LANES]
        out_ref[pl.ds(base + 4, chunk, stride=MESSAGE), :] = label_ref[pl.ds(block * chunk, chunk), :]


def halves(values):
    high = values.astype(BF16)
    return jnp.concatenate([high, (values - high.astype(F32)).astype(BF16)], axis=1)


def merge_kernel(got_ref, out_ref):
    source = lax.broadcasted_iota(jnp.int32, (8, 8, LANES), 0)
    lane = lax.broadcasted_iota(jnp.int32, (8, 8, LANES), 2)
    labels = []
    for k in range(GRP // 8):
        rows = jnp.where(lane // RCAP == source, got_ref[8 * k : 8 * k + 8, 64:72, :], 0.0)
        labels.append(jnp.sum(rows, axis=0)[0:1, :])
    pick = one_hot(jnp.concatenate(labels, axis=1).astype(jnp.int32), 0, RROWS)
    for h in range(2):
        values = got_ref[:, 16 * h : 16 * h + 16, :].reshape(GRP * RCAP, LANES)
        both = jnp.dot(pick, halves(values), preferred_element_type=F32)
        out_ref[h, 0:64, :] = both[:, :LANES] + both[:, LANES:]
        out_ref[h, 64:80, :] = jnp.sum(got_ref[:, 32 + 16 * h : 48 + 16 * h, :], axis=0)


def owner_kernel(got_ref, out_ref):
    labels = jnp.transpose(got_ref[pl.ds(4, DEVICES, stride=MESSAGE), :])[0:8, :].astype(jnp.int32)
    total = None
    for p in range(QCAP):
        pick = one_hot(labels[p : p + 1, :], 0, QROWS)
        values = jnp.concatenate([got_ref[pl.ds(2 * p + h, DEVICES, stride=MESSAGE), :] for h in range(2)], axis=1)
        part = sums(pick, halves(values))
        total = part if total is None else total + part
    out_ref[...] = total


def finish_kernel(own_ref, other_ref, own_rem_ref, other_rem_ref, rem_ref, tower_ref):
    group = lax.axis_index("x") * NY + lax.axis_index("y")

    def place(own, other, left, right):
        rem_ref[:, left] = own[0][...]
        rem_ref[:, right] = other[0][...]
        for j in range(GRP):
            rows = pl.ds(pl.multiple_of(jnp.bitwise_xor(group, j) * TROWS, TROWS), TROWS)
            tower_ref[rows, left] = own[1][j * TROWS : (j + 1) * TROWS, :]
            tower_ref[rows, right] = other[1][j * TROWS : (j + 1) * TROWS, :]

    low, high = slice(0, LANES), slice(LANES, E)

    @pl.when(lax.axis_index("c") == 0)
    def _():
        place((own_rem_ref, own_ref), (other_rem_ref, other_ref), low, high)

    @pl.when(lax.axis_index("c") == 1)
    def _():
        place((own_rem_ref, own_ref), (other_rem_ref, other_ref), high, low)


def shift(value, axis, size, by):
    return lax.ppermute(value, axis, [(i, (i + by) % size) for i in range(size)])


def swap(value, axis, size, bit):
    return lax.ppermute(value, axis, [(i, i ^ bit) for i in range(size)])


def local(
    pooled_grad,
    lookup_bag,
    saved_quotient,
    saved_remainder,
    quotient_slot,
    quotient_rows,
    remainder_slot,
    remainder_rows,
    tower_inputs,
    tower_cotangent,
):
    parts = pltpu.VMEM((LOOK, 2 * E), BF16)
    pieces = call(
        small_kernel,
        jax.ShapeDtypeStruct((GRP, PIECE, LANES), F32),
        (lookup_bag, lookup_bag, pooled_grad, saved_quotient, remainder_slot, remainder_rows, tower_inputs, tower_cotangent),
        [SMEM] + [VMEM] * 7,
        [parts],
        flops=2 * 10**9,
        nbytes=3 * 10**6,
    )
    got = lax.all_to_all(pieces, ("x", "y"), split_axis=0, concat_axis=0, tiled=True)
    label_rows = jnp.pad(quotient_rows.reshape(DEVICES, QCAP).astype(F32), ((0, 0), (0, LANES - QCAP)))
    outgoing = call(
        large_kernel,
        jax.ShapeDtypeStruct((DEVICES * MESSAGE, LANES), F32),
        (lookup_bag, lookup_bag, pooled_grad, saved_remainder, quotient_slot, label_rows),
        [SMEM] + [VMEM] * 5,
        [parts],
        flops=8 * 10**9,
        nbytes=5 * 10**6,
    )
    arrived = lax.all_to_all(
        outgoing.reshape(DEVICES, 1, MESSAGE * LANES), AXES, split_axis=0, concat_axis=0, tiled=True
    )
    merged = call(
        merge_kernel,
        jax.ShapeDtypeStruct((2, RROWS + TROWS, LANES), F32),
        (got,),
        [VMEM],
        flops=10**8,
        nbytes=2 * 10**6,
    )
    core = lax.axis_index("c")
    keep = lax.dynamic_index_in_dim(merged, core, 0, keepdims=False)
    give = lax.dynamic_index_in_dim(merged, 1 - core, 0, keepdims=False)
    keep = keep + swap(give, "c", NC, 1)
    keep = keep + shift(keep, "z", NZ, 1) + shift(keep, "z", NZ, -1)
    keep = keep + shift(keep, "z", NZ, 3) + shift(keep, "z", NZ, -3) + shift(keep, "z", NZ, 6)
    remainder_half, tower_half = keep[:RROWS], keep[RROWS:]
    for bit in (1, 2, 4):
        tower_half = jnp.concatenate([tower_half, swap(tower_half, "y", NY, bit)], axis=0)
    for bit in (1, 2):
        tower_half = jnp.concatenate([tower_half, swap(tower_half, "x", NX, bit)], axis=0)
    remainder_grad, tower_grad = call(
        finish_kernel,
        (jax.ShapeDtypeStruct((RROWS, E), F32), jax.ShapeDtypeStruct((HID, E), F32)),
        (tower_half, swap(tower_half, "c", NC, 1), remainder_half, swap(remainder_half, "c", NC, 1)),
        [VMEM] * 4,
        flops=10**6,
        nbytes=10**6,
    )
    quotient_grad = call(
        owner_kernel,
        jax.ShapeDtypeStruct((QROWS, E), F32),
        (arrived.reshape(DEVICES * MESSAGE, LANES),),
        [VMEM],
        flops=10**9,
        nbytes=3 * 10**6,
    )
    return (quotient_grad, remainder_grad, tower_grad)


def solution(mesh):
    fine = Mesh(mesh.devices.reshape(NX, NY, NZ, NC), AXES)
    rows = P(AXES, None)
    return jax.shard_map(
        local,
        mesh=fine,
        in_specs=(rows,) * 10,
        out_specs=(rows, P(("x", "y"), None), P()),
        check_vma=False,
    )
```

time: 748 us -> 206 us (0.28)
  the two profiles are of different devices: /device:TPU:2 before, /device:TPU:45 now
where the time goes in v1:
time: 206 us; the launch traced here: 205 us
  starting transfers between devices  95.9 us (47%)
  waiting for transfers between devices  89.7 us (44%)
  Pallas kernels  11.9 us (6%)
  local copies, waits for them, and re-layouts  6.52 us (3%)
    ppermute x5, waiting for transfers between devices, shift(): lax.ppermute(value, axis, [(i, (i + by) % size) for i in range(size)])  54.3 us
    all_to_all x1, starting transfers between devices, local(): lax.all_to_all(outgoing.reshape(DEVICES, 1, MESSAGE * LANES), AXES, split...  31.4 us
    ppermute x8, starting transfers between devices, swap(): return lax.ppermute(value, axis, [(i, i ^ bit) for i in range(size)])  30.3 us
    ppermute x5, starting transfers between devices, shift(): lax.ppermute(value, axis, [(i, (i + by) % size) for i in range(size)])  24.9 us
    ppermute x8, waiting for transfers between devices, swap(): return lax.ppermute(value, axis, [(i, i ^ bit) for i in range(size)])  17.9 us
    all_to_all x1, waiting for transfers between devices, local(): lax.all_to_all(pieces, ('x', 'y'), split_axis=0, concat_axis=0, tiled=True)  17.5 us
    pallas_call x5, Pallas kernels, call(): pl.pallas_call(body, out_shape=out_shape, in_specs=specs, out_specs=jax.t...  11.9 us
    all_to_all x1, starting transfers between devices, local(): lax.all_to_all(pieces, ('x', 'y'), split_axis=0, concat_axis=0, tiled=True)  9.27 us
  transfers between devices with their start and end apart: 15, of which 11 were waited for; matrix products, arithmetic and copies ran while one was open for 0% of the time, Pallas kernels for 3%

profile of v1, /device:TPU:45, one launch (start us, length us, event | category | flops | bytes accessed | tf_op | source)
XLA Modules:
  0.0 205.1 jit_solution(7077500791421251626)
XLA Ops:
  0.6 0.0 copy-start
  0.6 1.2 copy-done
  1.9 0.0 copy-start.2
  1.9 1.0 copy-done.2
  2.9 0.0 copy-start.4
  2.9 0.9 copy-done.4
  3.8 0.0 copy-start.5
  3.8 0.8 copy-done.5
  4.6 0.0 copy-start.6
  4.6 0.7 copy-done.6
  5.3 0.0 copy-start.7
  5.3 0.7 copy-done.7
  6.0 0.0 copy-start.10
  6.0 0.7 copy-done.10
  6.7 3.5 %shard_map.123 = f32[32,72,128]{2,1,0:T(8,128)} custom-call(s32[1,2048]{1,0:T(1,128)S(1)} %copy-done.7, s32[1,2048]{1,0:T(1,128)S(1)} %copy-done.7, bf16[1024,256]{1,0:T(8,128)(2,1)S(1)} %copy-done.2, bf16[2048,256]{1,0:T(8,128)(2,1)S(1)} %copy-done, s32[1,2048]{1,0:T(1,128)S(1)} %copy-done.6, s32[1,512]{1,0:T(1,128)S(1)} %copy-done.10, ...), custom_call_target="tpu_custom_call" | custom-call | flops 2000000000 | bytes 3000000 | tf_op jit(solution)/shard_map/pallas_call | solution.py:32
  10.2 0.0 copy-start.11
  10.2 0.0 copy-start.1
  10.2 0.0 copy-start.3
  10.2 0.0 copy-start.8
  10.2 0.0 copy-start.9
  10.2 9.3 %all-to-all-start.1 = ((f32[32,72,128]{2,1,0:T(8,128)}), f32[32,72,128]{2,1,0:T(8,128)S(1)}, u32[]{:S(2)}, u32[]{:S(2)}) async-start(f32[32,72,128]{2,1,0:T(8,128)} %shard_map.123), calls=%async_computation.1 | async-start | bytes 2359296 | tf_op jit(solution)/shard_map/all_to_all | solution.py:189
  19.5 0.0 copy-done.11
  19.5 0.3 convert_element_type.9
  19.9 0.0 copy-done.1
  19.9 0.0 copy-done.3
  19.9 0.0 copy-done.8
  20.0 0.0 copy-done.9
  20.0 6.0 %shard_map.121 = f32[3840,128]{1,0:T(8,128)} custom-call(s32[1,2048]{1,0:T(1,128)S(1)} %copy-done.8, s32[1,2048]{1,0:T(1,128)S(1)} %copy-done.8, bf16[1024,256]{1,0:T(8,128)(2,1)S(1)} %copy-done.3, bf16[2048,256]{1,0:T(8,128)(2,1)S(1)} %copy-done.1, s32[1,2048]{1,0:T(1,128)S(1)} %copy-done.9, f32[768,128]{1,0:T(8,128)S(1)} %pad.4.label_ref), custom_call_target="tpu_custom_call" | custom-call | flops 8000000000 | bytes 5000000 | tf_op jit(solution)/shard_map/pallas_call | solution.py:32
  25.9 17.5 %all-to-all-done.1.got_ref = f32[32,72,128]{2,1,0:T(8,128)S(1)} async-done(((f32[32,72,128]{2,1,0:T(8,128)}), f32[32,72,128]{2,1,0:T(8,128)S(1)}, u32[]{:S(2)}, u32[]{:S(2)}) %all-to-all-start.1) | async-done | bytes 1179680 | tf_op jit(solution)/shard_map/all_to_all | solution.py:189
  43.4 31.4 %all-to-all-start = ((f32[768,1,640]{2,1,0:T(1,128)}), f32[768,1,640]{2,1,0:T(1,128)S(1)}, u32[]{:S(2)}, u32[]{:S(2)}) async-start(f32[768,1,640]{2,1,0:T(1,128)} %bitcast), calls=%async_computation | async-start | bytes 3932160 | tf_op jit(solution)/shard_map/all_to_all | solution.py:200
  74.9 0.2 shard_map.124
  75.1 2.3 %collective-permute-start = (f32[80,128]{1,0:T(8,128)S(1)}, f32[80,128]{1,0:T(8,128)S(1)}, u32[]{:S(2)}, u32[]{:S(2)}) collective-permute-start(f32[80,128]{1,0:T(8,128)S(1)} %dynamic-slice_bitcast_fusion), channel_id=1, source_target_pairs={{0,1},{1,0},{2,3},{3,2},{4,5},{5,4},{6,7},{7,6},{8,9},{9,8},{10,11... | collective-permute-start | bytes 122888 | tf_op jit(solution)/shard_map/ppermute | solution.py:164
  77.4 0.8 collective-permute-done
  78.2 10.2 %collective-permute-start.2 = (f32[80,128]{1,0:T(8,128)S(1)}, f32[80,128]{1,0:T(8,128)S(1)}, u32[]{:S(2)}, u32[]{:S(2)}) collective-permute-start(f32[80,128]{1,0:T(8,128)S(1)} %bitcast_add_fusion), channel_id=1, source_target_pairs={{0,22},{2,0},{4,2},{6,4},{8,6},{10,8},{12,10},{14,12},{16,14},{18,... | collective-permute-start | bytes 122888 | tf_op jit(solution)/shard_map/ppermute | solution.py:160
  88.5 1.9 collective-permute-start.1
  90.4 44.2 %collective-permute-done.2 = f32[80,128]{1,0:T(8,128)S(1)} collective-permute-done((f32[80,128]{1,0:T(8,128)S(1)}, f32[80,128]{1,0:T(8,128)S(1)}, u32[]{:S(2)}, u32[]{:S(2)}) %collective-permute-start.2) | collective-permute-done | bytes 40992 | tf_op jit(solution)/shard_map/ppermute | solution.py:160
  134.6 7.5 %collective-permute-done.1 = f32[80,128]{1,0:T(8,128)S(1)} collective-permute-done((f32[80,128]{1,0:T(8,128)S(1)}, f32[80,128]{1,0:T(8,128)S(1)}, u32[]{:S(2)}, u32[]{:S(2)}) %collective-permute-start.1) | collective-permute-done | bytes 40992 | tf_op jit(solution)/shard_map/ppermute | solution.py:160
  142.1 5.7 %collective-permute-start.5 = (f32[80,128]{1,0:T(8,128)S(1)}, f32[80,128]{1,0:T(8,128)S(1)}, u32[]{:S(2)}, u32[]{:S(2)}) collective-permute-start(f32[80,128]{1,0:T(8,128)S(1)} %add_add_fusion.1), channel_id=1, source_target_pairs={{0,12},{2,14},{4,16},{6,18},{8,20},{10,22},{12,0},{14,2},{16,4},{1... | collective-permute-start | bytes 122888 | tf_op jit(solution)/shard_map/ppermute | solution.py:160
  147.8 1.9 collective-permute-start.4
  149.8 5.2 %collective-permute-start.3 = (f32[80,128]{1,0:T(8,128)S(1)}, f32[80,128]{1,0:T(8,128)S(1)}, u32[]{:S(2)}, u32[]{:S(2)}) collective-permute-start(f32[80,128]{1,0:T(8,128)S(1)} %add_add_fusion.1), channel_id=1, source_target_pairs={{0,6},{2,8},{4,10},{6,12},{8,14},{10,16},{12,18},{14,20},{16,22},{... | collective-permute-start | bytes 122888 | tf_op jit(solution)/shard_map/ppermute | solution.py:160
  154.9 0.0 collective-permute-done.5
  154.9 0.0 collective-permute-done.4
  155.0 2.6 %collective-permute-done.3 = f32[80,128]{1,0:T(8,128)S(1)} collective-permute-done((f32[80,128]{1,0:T(8,128)S(1)}, f32[80,128]{1,0:T(8,128)S(1)}, u32[]{:S(2)}, u32[]{:S(2)}) %collective-permute-start.3) | collective-permute-done | bytes 40992 | tf_op jit(solution)/shard_map/ppermute | solution.py:160
  157.6 3.9 %collective-permute-start.6 = (f32[16,128]{1,0:T(8,128)S(1)}, f32[16,128]{1,0:T(8,128)S(1)}, u32[]{:S(2)}, u32[]{:S(2)}) collective-permute-start(f32[16,128]{1,0:T(8,128)S(1)} %get-tuple-element.11), channel_id=1, source_target_pairs={{0,24},{24,0},{48,72},{72,48},{96,120},{120,96},{144,168},{168,144... | collective-permute-start | bytes 24584 | tf_op jit(solution)/shard_map/ppermute | solution.py:164
  161.5 1.0 collective-permute-done.6
  162.5 2.7 %collective-permute-start.7 = (f32[32,128]{1,0:T(8,128)S(1)}, f32[32,128]{1,0:T(8,128)S(1)}, u32[]{:S(2)}, u32[]{:S(2)}) collective-permute-start(f32[32,128]{1,0:T(8,128)S(1)} %pad_maximum_fusion.2), channel_id=1, source_target_pairs={{0,48},{24,72},{48,0},{72,24},{96,144},{120,168},{144,96},{168,120... | collective-permute-start | bytes 49160 | tf_op jit(solution)/shard_map/ppermute | solution.py:164
  165.2 2.6 %collective-permute-done.7 = f32[32,128]{1,0:T(8,128)S(1)} collective-permute-done((f32[32,128]{1,0:T(8,128)S(1)}, f32[32,128]{1,0:T(8,128)S(1)}, u32[]{:S(2)}, u32[]{:S(2)}) %collective-permute-start.7) | collective-permute-done | bytes 16416 | tf_op jit(solution)/shard_map/ppermute | solution.py:164
  167.9 3.2 %collective-permute-start.8 = (f32[64,128]{1,0:T(8,128)S(1)}, f32[64,128]{1,0:T(8,128)S(1)}, u32[]{:S(2)}, u32[]{:S(2)}) collective-permute-start(f32[64,128]{1,0:T(8,128)S(1)} %pad_maximum_fusion.1), channel_id=1, source_target_pairs={{0,96},{24,120},{48,144},{72,168},{96,0},{120,24},{144,48},{168,72... | collective-permute-start | bytes 98312 | tf_op jit(solution)/shard_map/ppermute | solution.py:164
  171.1 5.4 %collective-permute-done.8 = f32[64,128]{1,0:T(8,128)S(1)} collective-permute-done((f32[64,128]{1,0:T(8,128)S(1)}, f32[64,128]{1,0:T(8,128)S(1)}, u32[]{:S(2)}, u32[]{:S(2)}) %collective-permute-start.8) | collective-permute-done | bytes 32800 | tf_op jit(solution)/shard_map/ppermute | solution.py:164
  176.4 3.5 %collective-permute-start.9 = (f32[128,128]{1,0:T(8,128)S(1)}, f32[128,128]{1,0:T(8,128)S(1)}, u32[]{:S(2)}, u32[]{:S(2)}) collective-permute-start(f32[128,128]{1,0:T(8,128)S(1)} %pad_maximum_fusion), channel_id=1, source_target_pairs={{0,192},{192,0},{384,576},{576,384},{1,193},{193,1},{385,577},{577... | collective-permute-start | bytes 196616 | tf_op jit(solution)/shard_map/ppermute | solution.py:164
  180.0 1.9 collective-permute-done.9
  181.9 2.5 %collective-permute-start.10 = (f32[256,128]{1,0:T(8,128)S(1)}, f32[256,128]{1,0:T(8,128)S(1)}, u32[]{:S(2)}, u32[]{:S(2)}) collective-permute-start(f32[256,128]{1,0:T(8,128)S(1)} %get-tuple-element.7), channel_id=1, source_target_pairs={{0,384},{192,576},{384,0},{576,192},{1,385},{193,577},{385,1},{577... | collective-permute-start | bytes 393224 | tf_op jit(solution)/shard_map/ppermute | solution.py:164
  184.5 4.9 %collective-permute-done.10 = f32[256,128]{1,0:T(8,128)S(1)} collective-permute-done((f32[256,128]{1,0:T(8,128)S(1)}, f32[256,128]{1,0:T(8,128)S(1)}, u32[]{:S(2)}, u32[]{:S(2)}) %collective-permute-start.10) | collective-permute-done | bytes 131104 | tf_op jit(solution)/shard_map/ppermute | solution.py:164
  189.4 10.3 %collective-permute-start.11 = (f32[512,128]{1,0:T(8,128)S(1)}, f32[512,128]{1,0:T(8,128)S(1)}, u32[]{:S(2)}, u32[]{:S(2)}) collective-permute-start(f32[512,128]{1,0:T(8,128)S(1)} %constant_dynamic-update-slice_fusion.5.own_ref), channel_id=1, source_target_pairs={{0,1},{1,0},{2,3},{3,2},{4,5},{5,4},{6,7},{7,6},{8,9},{9,8},{10,11... | collective-permute-start | bytes 786440 | tf_op jit(solution)/shard_map/ppermute | solution.py:164
  199.7 1.9 collective-permute-start.12
  201.7 1.2 collective-permute-done.12.other_rem_ref
  202.8 0.0 collective-permute-done.11.other_ref
  202.8 0.9 shard_map.125
  203.7 0.0 all-to-all-done
  203.7 1.4 shard_map.122
  (16 shorter events, 0.2 us)
Async XLA Ops:
  0.6 1.2 copy-start
  1.9 1.0 copy-start.2
  2.9 0.9 copy-start.4
  3.8 0.8 copy-start.5
  4.6 0.7 copy-start.6
  5.3 0.7 copy-start.7
  6.0 0.7 copy-start.10
  10.2 9.3 %copy-start.11 = (s32[1,1536]{1,0:T(1,128)S(1)}, s32[1,1536]{1,0:T(1,128)}, u32[]{:S(2)}) copy-start(s32[1,1536]{1,0:T(1,128)} %param.15) | copy-start | bytes 18436
  10.2 9.7 %copy-start.1 = (bf16[2048,256]{1,0:T(8,128)(2,1)S(1)}, bf16[2048,256]{1,0:T(8,128)(2,1)}, u32[]{:S(2)}) copy-start(bf16[2048,256]{1,0:T(8,128)(2,1)} %saved_ref.2) | copy-start | bytes 3145732
  10.2 9.7 %copy-start.3 = (bf16[1024,256]{1,0:T(8,128)(2,1)S(1)}, bf16[1024,256]{1,0:T(8,128)(2,1)}, u32[]{:S(2)}) copy-start(bf16[1024,256]{1,0:T(8,128)(2,1)} %pooled_ref.3) | copy-start | bytes 1572868
  10.2 9.7 %copy-start.8 = (s32[1,2048]{1,0:T(1,128)S(1)}, s32[1,2048]{1,0:T(1,128)}, u32[]{:S(2)}) copy-start(s32[1,2048]{1,0:T(1,128)} %bag_ref.3) | copy-start | bytes 24580
  10.2 9.7 %copy-start.9 = (s32[1,2048]{1,0:T(1,128)S(1)}, s32[1,2048]{1,0:T(1,128)}, u32[]{:S(2)}) copy-start(s32[1,2048]{1,0:T(1,128)} %slot_ref.2) | copy-start | bytes 24580
  10.2 33.2 %all-to-all-start.1 = ((f32[32,72,128]{2,1,0:T(8,128)}), f32[32,72,128]{2,1,0:T(8,128)S(1)}, u32[]{:S(2)}, u32[]{:S(2)}) async-start(f32[32,72,128]{2,1,0:T(8,128)} %shard_map.123), calls=%async_computation.1 | async-start | bytes 2359296 | tf_op jit(solution)/shard_map/all_to_all | solution.py:189
  43.4 160.2 %all-to-all-start = ((f32[768,1,640]{2,1,0:T(1,128)}), f32[768,1,640]{2,1,0:T(1,128)S(1)}, u32[]{:S(2)}, u32[]{:S(2)}) async-start(f32[768,1,640]{2,1,0:T(1,128)} %bitcast), calls=%async_computation | async-start | bytes 3932160 | tf_op jit(solution)/shard_map/all_to_all | solution.py:200
  75.1 3.1 %collective-permute-start = (f32[80,128]{1,0:T(8,128)S(1)}, f32[80,128]{1,0:T(8,128)S(1)}, u32[]{:S(2)}, u32[]{:S(2)}) collective-permute-start(f32[80,128]{1,0:T(8,128)S(1)} %dynamic-slice_bitcast_fusion), channel_id=1, source_target_pairs={{0,1},{1,0},{2,3},{3,2},{4,5},{5,4},{6,7},{7,6},{8,9},{9,8},{10,11... | collective-permute-start | bytes 122888 | tf_op jit(solution)/shard_map/ppermute | solution.py:164
  78.2 56.3 %collective-permute-start.2 = (f32[80,128]{1,0:T(8,128)S(1)}, f32[80,128]{1,0:T(8,128)S(1)}, u32[]{:S(2)}, u32[]{:S(2)}) collective-permute-start(f32[80,128]{1,0:T(8,128)S(1)} %bitcast_add_fusion), channel_id=1, source_target_pairs={{0,22},{2,0},{4,2},{6,4},{8,6},{10,8},{12,10},{14,12},{16,14},{18,... | collective-permute-start | bytes 122888 | tf_op jit(solution)/shard_map/ppermute | solution.py:160
  88.5 53.6 %collective-permute-start.1 = (f32[80,128]{1,0:T(8,128)S(1)}, f32[80,128]{1,0:T(8,128)S(1)}, u32[]{:S(2)}, u32[]{:S(2)}) collective-permute-start(f32[80,128]{1,0:T(8,128)S(1)} %bitcast_add_fusion), channel_id=1, source_target_pairs={{0,2},{2,4},{4,6},{6,8},{8,10},{10,12},{12,14},{14,16},{16,18},{18... | collective-permute-start | bytes 122888 | tf_op jit(solution)/shard_map/ppermute | solution.py:160
  142.1 12.8 %collective-permute-start.5 = (f32[80,128]{1,0:T(8,128)S(1)}, f32[80,128]{1,0:T(8,128)S(1)}, u32[]{:S(2)}, u32[]{:S(2)}) collective-permute-start(f32[80,128]{1,0:T(8,128)S(1)} %add_add_fusion.1), channel_id=1, source_target_pairs={{0,12},{2,14},{4,16},{6,18},{8,20},{10,22},{12,0},{14,2},{16,4},{1... | collective-permute-start | bytes 122888 | tf_op jit(solution)/shard_map/ppermute | solution.py:160
  147.8 7.1 %collective-permute-start.4 = (f32[80,128]{1,0:T(8,128)S(1)}, f32[80,128]{1,0:T(8,128)S(1)}, u32[]{:S(2)}, u32[]{:S(2)}) collective-permute-start(f32[80,128]{1,0:T(8,128)S(1)} %add_add_fusion.1), channel_id=1, source_target_pairs={{0,18},{2,20},{4,22},{6,0},{8,2},{10,4},{12,6},{14,8},{16,10},{18,... | collective-permute-start | bytes 122888 | tf_op jit(solution)/shard_map/ppermute | solution.py:160
  149.8 7.8 %collective-permute-start.3 = (f32[80,128]{1,0:T(8,128)S(1)}, f32[80,128]{1,0:T(8,128)S(1)}, u32[]{:S(2)}, u32[]{:S(2)}) collective-permute-start(f32[80,128]{1,0:T(8,128)S(1)} %add_add_fusion.1), channel_id=1, source_target_pairs={{0,6},{2,8},{4,10},{6,12},{8,14},{10,16},{12,18},{14,20},{16,22},{... | collective-permute-start | bytes 122888 | tf_op jit(solution)/shard_map/ppermute | solution.py:160
  157.6 4.9 %collective-permute-start.6 = (f32[16,128]{1,0:T(8,128)S(1)}, f32[16,128]{1,0:T(8,128)S(1)}, u32[]{:S(2)}, u32[]{:S(2)}) collective-permute-start(f32[16,128]{1,0:T(8,128)S(1)} %get-tuple-element.11), channel_id=1, source_target_pairs={{0,24},{24,0},{48,72},{72,48},{96,120},{120,96},{144,168},{168,144... | collective-permute-start | bytes 24584 | tf_op jit(solution)/shard_map/ppermute | solution.py:164
  162.5 5.4 %collective-permute-start.7 = (f32[32,128]{1,0:T(8,128)S(1)}, f32[32,128]{1,0:T(8,128)S(1)}, u32[]{:S(2)}, u32[]{:S(2)}) collective-permute-start(f32[32,128]{1,0:T(8,128)S(1)} %pad_maximum_fusion.2), channel_id=1, source_target_pairs={{0,48},{24,72},{48,0},{72,24},{96,144},{120,168},{144,96},{168,120... | collective-permute-start | bytes 49160 | tf_op jit(solution)/shard_map/ppermute | solution.py:164
  167.9 8.6 %collective-permute-start.8 = (f32[64,128]{1,0:T(8,128)S(1)}, f32[64,128]{1,0:T(8,128)S(1)}, u32[]{:S(2)}, u32[]{:S(2)}) collective-permute-start(f32[64,128]{1,0:T(8,128)S(1)} %pad_maximum_fusion.1), channel_id=1, source_target_pairs={{0,96},{24,120},{48,144},{72,168},{96,0},{120,24},{144,48},{168,72... | collective-permute-start | bytes 98312 | tf_op jit(solution)/shard_map/ppermute | solution.py:164
  176.4 5.5 %collective-permute-start.9 = (f32[128,128]{1,0:T(8,128)S(1)}, f32[128,128]{1,0:T(8,128)S(1)}, u32[]{:S(2)}, u32[]{:S(2)}) collective-permute-start(f32[128,128]{1,0:T(8,128)S(1)} %pad_maximum_fusion), channel_id=1, source_target_pairs={{0,192},{192,0},{384,576},{576,384},{1,193},{193,1},{385,577},{577... | collective-permute-start | bytes 196616 | tf_op jit(solution)/shard_map/ppermute | solution.py:164
  181.9 7.5 %collective-permute-start.10 = (f32[256,128]{1,0:T(8,128)S(1)}, f32[256,128]{1,0:T(8,128)S(1)}, u32[]{:S(2)}, u32[]{:S(2)}) collective-permute-start(f32[256,128]{1,0:T(8,128)S(1)} %get-tuple-element.7), channel_id=1, source_target_pairs={{0,384},{192,576},{384,0},{576,192},{1,385},{193,577},{385,1},{577... | collective-permute-start | bytes 393224 | tf_op jit(solution)/shard_map/ppermute | solution.py:164
  189.4 13.4 %collective-permute-start.11 = (f32[512,128]{1,0:T(8,128)S(1)}, f32[512,128]{1,0:T(8,128)S(1)}, u32[]{:S(2)}, u32[]{:S(2)}) collective-permute-start(f32[512,128]{1,0:T(8,128)S(1)} %constant_dynamic-update-slice_fusion.5.own_ref), channel_id=1, source_target_pairs={{0,1},{1,0},{2,3},{3,2},{4,5},{5,4},{6,7},{7,6},{8,9},{9,8},{10,11... | collective-permute-start | bytes 786440 | tf_op jit(solution)/shard_map/ppermute | solution.py:164
  199.7 3.1 %collective-permute-start.12 = (f32[64,128]{1,0:T(8,128)S(1)}, f32[64,128]{1,0:T(8,128)S(1)}, u32[]{:S(2)}, u32[]{:S(2)}) collective-permute-start(f32[64,128]{1,0:T(8,128)S(1)} %slice.9.own_rem_ref), channel_id=1, source_target_pairs={{0,1},{1,0},{2,3},{3,2},{4,5},{5,4},{6,7},{7,6},{8,9},{9,8},{10,11... | collective-permute-start | bytes 98312 | tf_op jit(solution)/shard_map/ppermute | solution.py:164

commit v2 on v1

v2 whole, which is shorter than its diff:
```python
import jax
import jax.numpy as jnp
from jax import lax
from jax.experimental import pallas as pl
from jax.experimental.pallas import tpu as pltpu
from jax.sharding import Mesh
from jax.sharding import PartitionSpec as P

E = 256
LANES = 128
LOOK = 2048
BAGS = 1024
QCAP = 2
RCAP = 16
QROWS = 256
RROWS = 64
NX, NY, NZ, NC = 4, 8, 12, 2
GRP = NX * NY
DEVICES = GRP * NZ * NC
HID = 512
TROWS = HID // GRP
PIECE = 72
PLANE = NX * NC
SHEET = NY * NZ
CHAIN = 96
SUMS = RROWS + TROWS
F32 = jnp.float32
BF16 = jnp.bfloat16
AXES = ("x", "y", "z", "c")
VMEM = pl.BlockSpec(memory_space=pltpu.VMEM)
SMEM = pl.BlockSpec(memory_space=pltpu.SMEM)
ANY = pl.BlockSpec(memory_space=pl.ANY)


def call(body, out_shape, inputs, specs, scratch=(), flops=0, nbytes=0, room=32):
    return pl.pallas_call(
        body,
        out_shape=out_shape,
        in_specs=specs,
        out_specs=jax.tree.map(lambda _: VMEM, out_shape),
        scratch_shapes=list(scratch),
        compiler_params=pltpu.CompilerParams(vmem_limit_bytes=room * 1024 * 1024),
        cost_estimate=pl.CostEstimate(flops=flops, bytes_accessed=nbytes, transcendentals=0),
    )(*inputs)


def split_terms(bag_smem, bag_ref, pooled_ref, saved_ref, parts_ref):
    lane = lax.broadcasted_iota(jnp.int32, (LANES, LANES), 1)
    for block in range(LOOK // LANES):
        rows = pl.ds(block * LANES, LANES)
        first = jnp.minimum(bag_smem[0, block * LANES] // 16 * 16, BAGS - 2 * LANES)
        first = pl.multiple_of(first, 16)
        row = bag_ref[0:1, block * LANES : (block + 1) * LANES] - first
        column = jnp.transpose(jnp.broadcast_to(row, (LANES, LANES)).astype(F32)).astype(jnp.int32)
        pick = jnp.concatenate([column == lane, column == lane + LANES], axis=1)
        pick = jnp.where(pick, 1.0, 0.0).astype(BF16)
        gathered = jnp.dot(pick, pooled_ref[pl.ds(first, 2 * LANES), :], preferred_element_type=F32)
        terms = gathered * saved_ref[rows, :].astype(F32)
        high = terms.astype(BF16)
        parts_ref[rows, 0:E] = high
        parts_ref[rows, E:] = (terms - high.astype(F32)).astype(BF16)


def one_hot(index_row, first, count, step=1):
    number = lax.broadcasted_iota(jnp.int32, (count, index_row.shape[1]), 0) * step + first
    return jnp.where(number == index_row, 1.0, 0.0).astype(BF16)


def sums(pick, parts):
    both = jnp.dot(pick, parts, preferred_element_type=F32)
    return both[:, :E] + both[:, E:]


def small_kernel(
    bag_smem, bag_ref, slot_ref, rows_ref, qrows_ref, pooled_hbm, saved_hbm, tin_hbm, tcot_hbm, out_ref,
    pooled_ref, saved_ref, tin_ref, tcot_ref, parts_ref, arrivals,
):
    pairs = ((tin_hbm, tin_ref), (tcot_hbm, tcot_ref), (pooled_hbm, pooled_ref), (saved_hbm, saved_ref))
    copies = [pltpu.make_async_copy(src, dst, arrivals.at[k]) for k, (src, dst) in enumerate(pairs)]
    for copy in copies:
        copy.start()
    copies[0].wait()
    copies[1].wait()
    tower = lax.dot_general(tin_ref[...], tcot_ref[...], (((0,), (0,)), ((), ())), preferred_element_type=F32)
    tower = tower.reshape(GRP, TROWS, E)
    out_ref[:, 32:48, :] = tower[:, :, :LANES]
    out_ref[:, 48:64, :] = tower[:, :, LANES:]
    labels = jnp.broadcast_to(rows_ref[...], (GRP, GRP * RCAP))
    slot = lax.broadcasted_iota(jnp.int32, (GRP, GRP * RCAP), 1)
    group = lax.broadcasted_iota(jnp.int32, (GRP, GRP * RCAP), 0)
    labels = jnp.where(slot // RCAP == group, labels, 0).astype(F32).astype(BF16)
    slot = lax.broadcasted_iota(jnp.int32, (GRP * RCAP, LANES), 0)
    lane = lax.broadcasted_iota(jnp.int32, (GRP * RCAP, LANES), 1)
    spread = jnp.where(slot % RCAP == lane % RCAP, 1.0, 0.0).astype(BF16)
    labels = jnp.dot(labels, spread, preferred_element_type=F32)
    count = DEVICES * QCAP
    slot = lax.broadcasted_iota(jnp.int32, (GRP, count), 1)
    group = lax.broadcasted_iota(jnp.int32, (GRP, count), 0)
    onward = jnp.where(slot // (count // GRP) == group, jnp.broadcast_to(qrows_ref[...], (GRP, count)), 0).astype(F32).astype(BF16)
    slot = lax.broadcasted_iota(jnp.int32, (count, LANES), 0)
    lane = lax.broadcasted_iota(jnp.int32, (count, LANES), 1)
    spread = jnp.where(slot % (count // GRP) == lane, 1.0, 0.0).astype(BF16)
    onward = jnp.dot(onward, spread, preferred_element_type=F32)
    line = lax.broadcasted_iota(jnp.int32, (GRP, 8, LANES), 1)
    out_ref[:, 64:72, :] = jnp.where(line == 0, labels[:, None, :], onward[:, None, :])
    copies[2].wait()
    copies[3].wait()
    split_terms(bag_smem, bag_ref, pooled_ref, saved_ref, parts_ref)
    slots = slot_ref[...]
    for half in range(2):
        found = sums(one_hot(slots, half * 256, 256), parts_ref[...]).reshape(GRP // 2, RCAP, E)
        groups = pl.ds(half * (GRP // 2), GRP // 2)
        out_ref[groups, 0:16, :] = found[:, :, :LANES]
        out_ref[groups, 16:32, :] = found[:, :, LANES:]


def large_kernel(bag_smem, bag_ref, pooled_ref, saved_ref, slot_ref, out_ref, parts_ref):
    split_terms(bag_smem, bag_ref, pooled_ref, saved_ref, parts_ref)
    slots = slot_ref[...]
    row = lax.broadcasted_iota(jnp.int32, (2 * SHEET, LOOK), 0)
    home = row % SHEET * 4 + row // SHEET
    for block in range(PLANE):
        first = block // NC * (4 * SHEET) + block % NC * 2
        pick = jnp.where(home == slots - first, 1.0, 0.0).astype(BF16)
        found = sums(pick, parts_ref[...])
        for h in range(2):
            out_ref[block, h * 2 * SHEET : (h + 1) * 2 * SHEET, :] = found[:, h * LANES : (h + 1) * LANES]


def turn_kernel(got_ref, out_ref):
    for source in range(PLANE):
        for h in range(2):
            for p in range(QCAP):
                rows = pl.ds(h * 16 + source * QCAP + p, SHEET, stride=32)
                first = (h * QCAP + p) * SHEET
                out_ref[rows, :] = got_ref[source, first : first + SHEET, :]


def halves(values):
    high = values.astype(BF16)
    return jnp.concatenate([high, (values - high.astype(F32)).astype(BF16)], axis=1)


def merge_kernel(got_ref, keep_ref, give_ref, onward_ref):
    source = lax.broadcasted_iota(jnp.int32, (8, 8, LANES), 0)
    lane = lax.broadcasted_iota(jnp.int32, (8, 8, LANES), 2)
    labels = []
    for k in range(GRP // 8):
        rows = jnp.where(lane // RCAP == source, got_ref[8 * k : 8 * k + 8, 64:72, :], 0.0)
        labels.append(jnp.sum(rows, axis=0)[0:1, :])
    pick = one_hot(jnp.concatenate(labels, axis=1).astype(jnp.int32), 0, RROWS)
    core = lax.axis_index("c")
    for h in range(2):
        values = got_ref[:, 16 * h : 16 * h + 16, :].reshape(GRP * RCAP, LANES)
        both = jnp.dot(pick, halves(values), preferred_element_type=F32)
        remainder = both[:, :LANES] + both[:, LANES:]
        tower = jnp.sum(got_ref[:, 32 + 16 * h : 48 + 16 * h, :], axis=0)
        for kept, ref in ((True, keep_ref), (False, give_ref)):

            @pl.when((core == h) == kept)
            def _(ref=ref, remainder=remainder, tower=tower):
                ref[0:RROWS, :] = remainder
                ref[RROWS:SUMS, :] = tower

    line = lax.broadcasted_iota(jnp.int32, (GRP, 8, LANES), 1)
    known = jnp.sum(jnp.where(line == 1, got_ref[:, 64:72, :], 0.0), axis=1).astype(BF16)
    group = lax.broadcasted_iota(jnp.int32, (GRP, LANES), 0)
    lane = lax.broadcasted_iota(jnp.int32, (GRP, LANES), 1)
    total = None
    for p in range(QCAP):
        spread = jnp.where(lane == group % NY * 16 + group // NY * 4 + core * 2 + p, 1.0, 0.0).astype(BF16)
        moved = lax.dot_general(known, spread, (((0,), (0,)), ((), ())), preferred_element_type=F32)
        row = lax.broadcasted_iota(jnp.int32, (LANES, LANES), 0)
        moved = jnp.where(row % QCAP == p, moved, 0.0)
        total = moved if total is None else total + moved
    onward_ref[...] = total
    z = lax.axis_index("z")
    for ref, c in ((keep_ref, core), (give_ref, 1 - core)):
        ref[SUMS:, :] = jnp.zeros((CHAIN - SUMS, LANES), F32)
        for i in range(NZ):
            first = lax.rem(z + i + NZ - 5, NZ) * 4 + c * 2
            at = SUMS + i % 4 * 3 + i // 4
            ref[at : at + 1, :] = onward_ref[pl.ds(first, 1), :] + onward_ref[pl.ds(first + 1, 1), :]


def near_kernel(up_ref, own_ref, down1_ref, down2_ref, out_ref):
    refs = (up_ref, own_ref, down1_ref, down2_ref)
    out_ref[0:SUMS, :] = sum(ref[0:SUMS, :] for ref in refs)
    out_ref[SUMS:, :] = jnp.zeros((CHAIN - SUMS, LANES), F32)
    for m in range(3):
        for e, ref in enumerate(refs):
            at = SUMS + 4 * m + e
            out_ref[at : at + 1, :] = ref[SUMS + 3 * e + m : SUMS + 3 * e + m + 1, :]


def pass_kernel(value_ref, after1_ref, after2_ref, out_ref):
    pass


def owner_kernel(got_ref, step0_ref, step1_ref, step2_ref, out_ref, label_ref):
    z = lax.axis_index("z")
    for m, ref in enumerate((step0_ref, step1_ref, step2_ref)):
        label_ref[4 * m : 4 * m + 4, :] = ref[SUMS + 4 * m : SUMS + 4 * m + 4, :]
    labels = [label_ref[pl.ds(lax.rem(z - source + 5 + NZ, NZ), 1), :] for source in range(NZ)]
    pick = one_hot(jnp.concatenate(labels, axis=1).astype(jnp.int32), 0, QROWS)
    for h in range(2):
        values = [
            got_ref[y * NZ + source, 16 * h : 16 * h + 16, :] for source in range(NZ) for y in range(NY)
        ]
        both = jnp.dot(pick, halves(jnp.concatenate(values, axis=0)), preferred_element_type=F32)
        out_ref[:, h * LANES : (h + 1) * LANES] = both[:, :LANES] + both[:, LANES:]


def finish_kernel(own_ref, other_ref, own_rem_ref, other_rem_ref, rem_ref, tower_ref):
    group = lax.axis_index("x") * NY + lax.axis_index("y")

    def place(own, other, left, right):
        rem_ref[:, left] = own[0][...]
        rem_ref[:, right] = other[0][...]
        for j in range(GRP):
            rows = pl.ds(pl.multiple_of(jnp.bitwise_xor(group, j) * TROWS, TROWS), TROWS)
            tower_ref[rows, left] = own[1][j * TROWS : (j + 1) * TROWS, :]
            tower_ref[rows, right] = other[1][j * TROWS : (j + 1) * TROWS, :]

    low, high = slice(0, LANES), slice(LANES, E)

    @pl.when(lax.axis_index("c") == 0)
    def _():
        place((own_rem_ref, own_ref), (other_rem_ref, other_ref), low, high)

    @pl.when(lax.axis_index("c") == 1)
    def _():
        place((own_rem_ref, own_ref), (other_rem_ref, other_ref), high, low)


def shift(value, by):
    return lax.ppermute(value, "z", [(i, (i + by) % NZ) for i in range(NZ)])


def swap(value, axis, bit):
    return lax.ppermute(value, axis, [(i, i ^ bit) for i in range(lax.axis_size(axis))])


def local(
    pooled_grad,
    lookup_bag,
    saved_quotient,
    saved_remainder,
    quotient_slot,
    quotient_rows,
    remainder_slot,
    remainder_rows,
    tower_inputs,
    tower_cotangent,
):
    parts = pltpu.VMEM((LOOK, 2 * E), BF16)
    pieces = call(
        small_kernel,
        jax.ShapeDtypeStruct((GRP, PIECE, LANES), F32),
        (lookup_bag, lookup_bag, remainder_slot, remainder_rows, quotient_rows, pooled_grad, saved_quotient, tower_inputs, tower_cotangent),
        [SMEM] + [VMEM] * 4 + [ANY] * 4,
        [
            pltpu.VMEM(pooled_grad.shape, BF16),
            pltpu.VMEM(saved_quotient.shape, BF16),
            pltpu.VMEM(tower_inputs.shape, BF16),
            pltpu.VMEM(tower_cotangent.shape, BF16),
            parts,
            pltpu.SemaphoreType.DMA((4,)),
        ],
        flops=2 * 10**9,
        nbytes=3 * 10**6,
        room=56,
    )
    got = lax.all_to_all(pieces, ("x", "y"), split_axis=0, concat_axis=0, tiled=True)
    outgoing = call(
        large_kernel,
        jax.ShapeDtypeStruct((PLANE, 4 * SHEET, LANES), F32),
        (lookup_bag, lookup_bag, pooled_grad, saved_remainder, quotient_slot),
        [SMEM] + [VMEM] * 4,
        [parts],
        flops=8 * 10**9,
        nbytes=5 * 10**6,
    )
    across = lax.all_to_all(outgoing, ("x", "c"), split_axis=0, concat_axis=0, tiled=True)

    chain = jax.ShapeDtypeStruct((CHAIN, LANES), F32)
    keep, give = call(
        merge_kernel,
        (chain, chain),
        (got,),
        [VMEM],
        [pltpu.VMEM((LANES, LANES), F32)],
        flops=10**8,
        nbytes=2 * 10**6,
    )
    keep = keep + swap(give, "c", 1)
    step = call(
        near_kernel,
        chain,
        (shift(keep, -1), keep, shift(keep, 1), shift(keep, 2)),
        [VMEM] * 4,
        flops=10**5,
        nbytes=10**5,
    )
    steps = (shift(step, -4), step, shift(step, 4))
    total = sum(value[:SUMS] for value in steps)

    turned = call(
        turn_kernel,
        jax.ShapeDtypeStruct((SHEET * 32, LANES), F32),
        (across,),
        [VMEM],
        flops=10**7,
        nbytes=4 * 10**6,
    )
    turned = pl.pallas_call(
        pass_kernel,
        out_shape=jax.ShapeDtypeStruct((SHEET * 32, LANES), F32),
        in_specs=[ANY] * 3,
        out_specs=ANY,
        input_output_aliases={0: 0},
    )(turned, steps[0], steps[2])
    arrived = lax.all_to_all(turned.reshape(SHEET, 32, LANES), ("y", "z"), split_axis=0, concat_axis=0, tiled=True)

    remainder_half, tower_half = total[:RROWS], total[RROWS:]
    for axis, bits in (("y", (1, 2, 4)), ("x", (1, 2))):
        for bit in bits:
            tower_half = jnp.concatenate([tower_half, swap(tower_half, axis, bit)], axis=0)
    remainder_grad, tower_grad = call(
        finish_kernel,
        (jax.ShapeDtypeStruct((RROWS, E), F32), jax.ShapeDtypeStruct((HID, E), F32)),
        (tower_half, swap(tower_half, "c", 1), remainder_half, swap(remainder_half, "c", 1)),
        [VMEM] * 4,
        flops=10**6,
        nbytes=10**6,
    )
    quotient_grad = call(
        owner_kernel,
        jax.ShapeDtypeStruct((QROWS, E), F32),
        (arrived, *steps),
        [VMEM] * 4,
        [pltpu.VMEM((16, LANES), F32)],
        flops=10**9,
        nbytes=3 * 10**6,
    )
    return (quotient_grad, remainder_grad, tower_grad)


def solution(mesh):
    fine = Mesh(mesh.devices.reshape(NX, NY, NZ, NC), AXES)
    rows = P(AXES, None)
    return jax.shard_map(
        local,
        mesh=fine,
        in_specs=(rows,) * 10,
        out_specs=(rows, P(("x", "y"), None), P()),
        check_vma=False,
    )
```

time: 206 us -> 164 us (0.80)
  the two profiles are of different devices: /device:TPU:45 before, /device:TPU:8 now
where the time goes in v2:
time: 164 us; the launch traced here: 163 us
  starting transfers between devices  84.3 us (51%)
  waiting for transfers between devices  60 us (37%)
  Pallas kernels  14.2 us (9%)
  local copies, waits for them, and re-layouts  3.04 us (2%)
    ppermute x8, starting transfers between devices, swap(): lax.ppermute(value, axis, [(i, i ^ bit) for i in range(lax.axis_size(axis...  28.9 us
    ppermute x5, starting transfers between devices, shift(): return lax.ppermute(value, 'z', [(i, (i + by) % NZ) for i in range(NZ)])  28.3 us
    all_to_all x1, waiting for transfers between devices, local(): lax.all_to_all(pieces, ('x', 'y'), split_axis=0, concat_axis=0, tiled=True)  22.6 us
    ppermute x8, waiting for transfers between devices, swap(): lax.ppermute(value, axis, [(i, i ^ bit) for i in range(lax.axis_size(axis...  18.4 us
    pallas_call x7, Pallas kernels, call(): pl.pallas_call(body, out_shape=out_shape, in_specs=specs, out_specs=jax.t...  14.2 us
    all_to_all x1, waiting for transfers between devices, local(): lax.all_to_all(turned.reshape(SHEET, 32, LANES), ('y', 'z'), split_axis=0...  13.3 us
    all_to_all x1, starting transfers between devices, local(): lax.all_to_all(pieces, ('x', 'y'), split_axis=0, concat_axis=0, tiled=True)  13.2 us
    all_to_all x1, starting transfers between devices, local(): lax.all_to_all(turned.reshape(SHEET, 32, LANES), ('y', 'z'), split_axis=0...  10.4 us
  transfers between devices with their start and end apart: 16, of which 12 were waited for; matrix products, arithmetic and copies ran while one was open for 0% of the time, Pallas kernels for 5%

profile of v2, /device:TPU:8, one launch (start us, length us, event | category | flops | bytes accessed | tf_op | source)
XLA Modules:
  0.0 162.7 jit_solution(15504747966513890165)
XLA Ops:
  0.6 5.2 %shard_map.123 = f32[32,72,128]{2,1,0:T(8,128)} custom-call(s32[1,2048]{1,0:T(1,128)} %bag_ref.3, s32[1,2048]{1,0:T(1,128)} %bag_ref.3, s32[1,2048]{1,0:T(1,128)} %slot_ref.3, s32[1,512]{1,0:T(1,128)} %rows_ref.1, s32[1,1536]{1,0:T(1,128)} %qrows_ref.1, bf16[1024,256]{1,0:T(8,128)(2,1)} %pooled_hbm.1, bf16[2048,256]{1,0:T(8,128)(2,1)} %saved_hbm.1, ...), custom_call_target="tpu_custom_call" | custom-call | flops 2000000000 | bytes 3000000 | tf_op jit(solution)/shard_map/pallas_call | solution.py:36
  5.9 0.0 copy-start.6
  5.9 0.0 copy-start.7
  5.9 0.0 copy-start.8
  5.9 0.0 copy-start.9
  5.9 13.2 %all-to-all-start.1 = ((f32[32,72,128]{2,1,0:T(8,128)}), f32[32,72,128]{2,1,0:T(8,128)S(1)}, u32[]{:S(2)}, u32[]{:S(2)}) async-start(f32[32,72,128]{2,1,0:T(8,128)} %shard_map.123), calls=%async_computation.1 | async-start | bytes 2359296 | tf_op jit(solution)/shard_map/all_to_all | solution.py:274
  19.1 0.0 copy-done.6
  19.1 0.0 copy-done.7
  19.1 0.0 copy-done.8
  19.1 0.0 copy-done.9
  19.2 4.6 %shard_map.121 = f32[8,384,128]{2,1,0:T(8,128)S(1)} custom-call(s32[1,2048]{1,0:T(1,128)S(1)} %copy-done.8, s32[1,2048]{1,0:T(1,128)S(1)} %copy-done.8, bf16[1024,256]{1,0:T(8,128)(2,1)S(1)} %copy-done.7, bf16[2048,256]{1,0:T(8,128)(2,1)S(1)} %copy-done.6, s32[1,2048]{1,0:T(1,128)S(1)} %copy-done.9), custom_call_target="tpu_custom_call" | custom-call | flops 8000000000 | bytes 5000000 | tf_op jit(solution)/shard_map/pallas_call | solution.py:36
  23.8 0.0 copy-start.1
  23.8 1.2 copy-done.1
  24.9 22.6 %all-to-all-done.1.got_ref = f32[32,72,128]{2,1,0:T(8,128)S(1)} async-done(((f32[32,72,128]{2,1,0:T(8,128)}), f32[32,72,128]{2,1,0:T(8,128)S(1)}, u32[]{:S(2)}, u32[]{:S(2)}) %all-to-all-start.1) | async-done | bytes 1179680 | tf_op jit(solution)/shard_map/all_to_all | solution.py:274
  47.5 3.6 %all-to-all-start = ((f32[8,384,128]{2,1,0:T(8,128)}), f32[8,384,128]{2,1,0:T(8,128)S(1)}, u32[]{:S(2)}, u32[]{:S(2)}) async-start(f32[8,384,128]{2,1,0:T(8,128)} %copy-done.1), calls=%async_computation | async-start | bytes 3145728 | tf_op jit(solution)/shard_map/all_to_all | solution.py:284
  51.1 0.7 shard_map.124
  51.8 2.3 %collective-permute-start = (f32[96,128]{1,0:T(8,128)S(1)}, f32[96,128]{1,0:T(8,128)S(1)}, u32[]{:S(2)}, u32[]{:S(2)}) collective-permute-start(f32[96,128]{1,0:T(8,128)S(1)} %get-tuple-element.8), channel_id=1, source_target_pairs={{0,1},{1,0},{2,3},{3,2},{4,5},{5,4},{6,7},{7,6},{8,9},{9,8},{10,11... | collective-permute-start | bytes 147464 | tf_op jit(solution)/shard_map/ppermute | solution.py:241
  54.1 0.9 collective-permute-done
  55.0 6.0 %collective-permute-start.3 = (f32[96,128]{1,0:T(8,128)S(1)}, f32[96,128]{1,0:T(8,128)S(1)}, u32[]{:S(2)}, u32[]{:S(2)}) collective-permute-start(f32[96,128]{1,0:T(8,128)S(1)} %add.9.own_ref), channel_id=1, source_target_pairs={{0,4},{2,6},{4,8},{6,10},{8,12},{10,14},{12,16},{14,18},{16,20},{1... | collective-permute-start | bytes 147464 | tf_op jit(solution)/shard_map/ppermute | solution.py:237
  61.0 4.3 %collective-permute-start.2 = (f32[96,128]{1,0:T(8,128)S(1)}, f32[96,128]{1,0:T(8,128)S(1)}, u32[]{:S(2)}, u32[]{:S(2)}) collective-permute-start(f32[96,128]{1,0:T(8,128)S(1)} %add.9.own_ref), channel_id=1, source_target_pairs={{0,2},{2,4},{4,6},{6,8},{8,10},{10,12},{12,14},{14,16},{16,18},{18... | collective-permute-start | bytes 147464 | tf_op jit(solution)/shard_map/ppermute | solution.py:237
  65.3 8.1 %collective-permute-start.1 = (f32[96,128]{1,0:T(8,128)S(1)}, f32[96,128]{1,0:T(8,128)S(1)}, u32[]{:S(2)}, u32[]{:S(2)}) collective-permute-start(f32[96,128]{1,0:T(8,128)S(1)} %add.9.own_ref), channel_id=1, source_target_pairs={{0,22},{2,0},{4,2},{6,4},{8,6},{10,8},{12,10},{14,12},{16,14},{18,... | collective-permute-start | bytes 147464 | tf_op jit(solution)/shard_map/ppermute | solution.py:237
  73.3 0.0 collective-permute-done.3.down2_ref
  73.3 0.5 collective-permute-done.2.down1_ref
  73.8 1.3 collective-permute-done.1.up_ref
  75.1 6.8 %collective-permute-start.5 = (f32[96,128]{1,0:T(8,128)S(1)}, f32[96,128]{1,0:T(8,128)S(1)}, u32[]{:S(2)}, u32[]{:S(2)}) collective-permute-start(f32[96,128]{1,0:T(8,128)S(1)} %shard_map.125.step1_ref), channel_id=1, source_target_pairs={{0,8},{2,10},{4,12},{6,14},{8,16},{10,18},{12,20},{14,22},{16,0},{... | collective-permute-start | bytes 147464 | tf_op jit(solution)/shard_map/ppermute | solution.py:237
  81.9 3.2 %collective-permute-start.4 = (f32[96,128]{1,0:T(8,128)S(1)}, f32[96,128]{1,0:T(8,128)S(1)}, u32[]{:S(2)}, u32[]{:S(2)}) collective-permute-start(f32[96,128]{1,0:T(8,128)S(1)} %shard_map.125.step1_ref), channel_id=1, source_target_pairs={{0,16},{2,18},{4,20},{6,22},{8,0},{10,2},{12,4},{14,6},{16,8},{18,... | collective-permute-start | bytes 147464 | tf_op jit(solution)/shard_map/ppermute | solution.py:237
  85.1 0.0 all-to-all-done.got_ref
  85.1 1.6 shard_map.122.value_ref
  86.7 0.0 copy-start
  86.7 1.2 copy-done
  87.9 0.0 collective-permute-done.5.after2_ref.step2_ref
  87.9 0.0 copy-start.2
  87.9 3.9 %collective-permute-done.4.after1_ref.step0_ref = f32[96,128]{1,0:T(8,128)S(1)} collective-permute-done((f32[96,128]{1,0:T(8,128)S(1)}, f32[96,128]{1,0:T(8,128)S(1)}, u32[]{:S(2)}, u32[]{:S(2)}) %collective-permute-start.4) | collective-permute-done | bytes 49184 | tf_op jit(solution)/shard_map/ppermute | solution.py:237
  91.8 0.0 copy-done.2
  91.8 0.0 copy-start.4
  91.8 0.6 copy-done.4
  92.4 0.0 copy-start.3
  92.4 0.0 copy-start.5
  92.4 10.4 %all-to-all-start.2 = ((f32[96,32,128]{2,1,0:T(8,128)}), f32[96,32,128]{2,1,0:T(8,128)S(1)}, u32[]{:S(2)}, u32[]{:S(2)}) async-start(f32[96,32,128]{2,1,0:T(8,128)} %bitcast.1), calls=%async_computation.2 | async-start | bytes 3145728 | tf_op jit(solution)/shard_map/all_to_all | solution.py:323
  102.9 0.0 copy-done.3
  102.9 0.0 copy-done.5
  102.9 2.6 %collective-permute-start.6 = (f32[16,128]{1,0:T(8,128)S(1)}, f32[16,128]{1,0:T(8,128)S(1)}, u32[]{:S(2)}, u32[]{:S(2)}) collective-permute-start(f32[16,128]{1,0:T(8,128)S(1)} %get-tuple-element.15), channel_id=1, source_target_pairs={{0,24},{24,0},{48,72},{72,48},{96,120},{120,96},{144,168},{168,144... | collective-permute-start | bytes 24584 | tf_op jit(solution)/shard_map/ppermute | solution.py:241
  105.5 3.0 %collective-permute-done.6 = f32[16,128]{1,0:T(8,128)S(1)} collective-permute-done((f32[16,128]{1,0:T(8,128)S(1)}, f32[16,128]{1,0:T(8,128)S(1)}, u32[]{:S(2)}, u32[]{:S(2)}) %collective-permute-start.6) | collective-permute-done | bytes 8224 | tf_op jit(solution)/shard_map/ppermute | solution.py:241
  108.5 4.3 %collective-permute-start.7 = (f32[32,128]{1,0:T(8,128)S(1)}, f32[32,128]{1,0:T(8,128)S(1)}, u32[]{:S(2)}, u32[]{:S(2)}) collective-permute-start(f32[32,128]{1,0:T(8,128)S(1)} %pad_maximum_fusion.2), channel_id=1, source_target_pairs={{0,48},{24,72},{48,0},{72,24},{96,144},{120,168},{144,96},{168,120... | collective-permute-start | bytes 49160 | tf_op jit(solution)/shard_map/ppermute | solution.py:241
  112.9 3.0 %collective-permute-done.7 = f32[32,128]{1,0:T(8,128)S(1)} collective-permute-done((f32[32,128]{1,0:T(8,128)S(1)}, f32[32,128]{1,0:T(8,128)S(1)}, u32[]{:S(2)}, u32[]{:S(2)}) %collective-permute-start.7) | collective-permute-done | bytes 16416 | tf_op jit(solution)/shard_map/ppermute | solution.py:241
  115.9 6.2 %collective-permute-start.8 = (f32[64,128]{1,0:T(8,128)S(1)}, f32[64,128]{1,0:T(8,128)S(1)}, u32[]{:S(2)}, u32[]{:S(2)}) collective-permute-start(f32[64,128]{1,0:T(8,128)S(1)} %pad_maximum_fusion.1), channel_id=1, source_target_pairs={{0,96},{24,120},{48,144},{72,168},{96,0},{120,24},{144,48},{168,72... | collective-permute-start | bytes 98312 | tf_op jit(solution)/shard_map/ppermute | solution.py:241
  122.1 3.6 %collective-permute-done.8 = f32[64,128]{1,0:T(8,128)S(1)} collective-permute-done((f32[64,128]{1,0:T(8,128)S(1)}, f32[64,128]{1,0:T(8,128)S(1)}, u32[]{:S(2)}, u32[]{:S(2)}) %collective-permute-start.8) | collective-permute-done | bytes 32800 | tf_op jit(solution)/shard_map/ppermute | solution.py:241
  125.7 5.0 %collective-permute-start.9 = (f32[128,128]{1,0:T(8,128)S(1)}, f32[128,128]{1,0:T(8,128)S(1)}, u32[]{:S(2)}, u32[]{:S(2)}) collective-permute-start(f32[128,128]{1,0:T(8,128)S(1)} %pad_maximum_fusion), channel_id=1, source_target_pairs={{0,192},{192,0},{384,576},{576,384},{1,193},{193,1},{385,577},{577... | collective-permute-start | bytes 196616 | tf_op jit(solution)/shard_map/ppermute | solution.py:241
  130.7 2.8 %collective-permute-done.9 = f32[128,128]{1,0:T(8,128)S(1)} collective-permute-done((f32[128,128]{1,0:T(8,128)S(1)}, f32[128,128]{1,0:T(8,128)S(1)}, u32[]{:S(2)}, u32[]{:S(2)}) %collective-permute-start.9) | collective-permute-done | bytes 65568 | tf_op jit(solution)/shard_map/ppermute | solution.py:241
  133.6 4.1 %collective-permute-start.10 = (f32[256,128]{1,0:T(8,128)S(1)}, f32[256,128]{1,0:T(8,128)S(1)}, u32[]{:S(2)}, u32[]{:S(2)}) collective-permute-start(f32[256,128]{1,0:T(8,128)S(1)} %get-tuple-element.11), channel_id=1, source_target_pairs={{0,384},{192,576},{384,0},{576,192},{1,385},{193,577},{385,1},{577... | collective-permute-start | bytes 393224 | tf_op jit(solution)/shard_map/ppermute | solution.py:241
  137.7 4.2 %collective-permute-done.10 = f32[256,128]{1,0:T(8,128)S(1)} collective-permute-done((f32[256,128]{1,0:T(8,128)S(1)}, f32[256,128]{1,0:T(8,128)S(1)}, u32[]{:S(2)}, u32[]{:S(2)}) %collective-permute-start.10) | collective-permute-done | bytes 131104 | tf_op jit(solution)/shard_map/ppermute | solution.py:241
  142.0 1.9 %collective-permute-start.11 = (f32[512,128]{1,0:T(8,128)S(1)}, f32[512,128]{1,0:T(8,128)S(1)}, u32[]{:S(2)}, u32[]{:S(2)}) collective-permute-start(f32[512,128]{1,0:T(8,128)S(1)} %constant_dynamic-update-slice_fusion.5.own_ref), channel_id=1, source_target_pairs={{0,1},{1,0},{2,3},{3,2},{4,5},{5,4},{6,7},{7,6},{8,9},{9,8},{10,11... | collective-permute-start | bytes 786440 | tf_op jit(solution)/shard_map/ppermute | solution.py:241
  143.9 2.4 %collective-permute-start.12 = (f32[64,128]{1,0:T(8,128)S(1)}, f32[64,128]{1,0:T(8,128)S(1)}, u32[]{:S(2)}, u32[]{:S(2)}) collective-permute-start(f32[64,128]{1,0:T(8,128)S(1)} %slice.24.own_rem_ref), channel_id=1, source_target_pairs={{0,1},{1,0},{2,3},{3,2},{4,5},{5,4},{6,7},{7,6},{8,9},{9,8},{10,11... | collective-permute-start | bytes 98312 | tf_op jit(solution)/shard_map/ppermute | solution.py:241
  146.3 0.8 collective-permute-done.12.other_rem_ref
  147.2 0.0 collective-permute-done.11.other_ref
  147.2 0.9 shard_map.128
  148.0 13.3 %all-to-all-done.2.got_ref = f32[96,32,128]{2,1,0:T(8,128)S(1)} async-done(((f32[96,32,128]{2,1,0:T(8,128)}), f32[96,32,128]{2,1,0:T(8,128)S(1)}, u32[]{:S(2)}, u32[]{:S(2)}) %all-to-all-start.2) | async-done | bytes 1572896 | tf_op jit(solution)/shard_map/all_to_all | solution.py:323
  161.4 1.3 shard_map.127
  (14 shorter events, 0.1 us)
Async XLA Ops:
  5.9 13.2 %copy-start.6 = (bf16[2048,256]{1,0:T(8,128)(2,1)S(1)}, bf16[2048,256]{1,0:T(8,128)(2,1)}, u32[]{:S(2)}) copy-start(bf16[2048,256]{1,0:T(8,128)(2,1)} %saved_ref.1) | copy-start | bytes 3145732
  5.9 13.2 %copy-start.7 = (bf16[1024,256]{1,0:T(8,128)(2,1)S(1)}, bf16[1024,256]{1,0:T(8,128)(2,1)}, u32[]{:S(2)}) copy-start(bf16[1024,256]{1,0:T(8,128)(2,1)} %pooled_hbm.1) | copy-start | bytes 1572868
  5.9 13.2 %copy-start.8 = (s32[1,2048]{1,0:T(1,128)S(1)}, s32[1,2048]{1,0:T(1,128)}, u32[]{:S(2)}) copy-start(s32[1,2048]{1,0:T(1,128)} %bag_ref.3) | copy-start | bytes 24580
  5.9 13.2 %copy-start.9 = (s32[1,2048]{1,0:T(1,128)S(1)}, s32[1,2048]{1,0:T(1,128)}, u32[]{:S(2)}) copy-start(s32[1,2048]{1,0:T(1,128)} %slot_ref.2) | copy-start | bytes 24580
  5.9 41.6 %all-to-all-start.1 = ((f32[32,72,128]{2,1,0:T(8,128)}), f32[32,72,128]{2,1,0:T(8,128)S(1)}, u32[]{:S(2)}, u32[]{:S(2)}) async-start(f32[32,72,128]{2,1,0:T(8,128)} %shard_map.123), calls=%async_computation.1 | async-start | bytes 2359296 | tf_op jit(solution)/shard_map/all_to_all | solution.py:274
  23.8 1.2 copy-start.1
  47.5 37.5 %all-to-all-start = ((f32[8,384,128]{2,1,0:T(8,128)}), f32[8,384,128]{2,1,0:T(8,128)S(1)}, u32[]{:S(2)}, u32[]{:S(2)}) async-start(f32[8,384,128]{2,1,0:T(8,128)} %copy-done.1), calls=%async_computation | async-start | bytes 3145728 | tf_op jit(solution)/shard_map/all_to_all | solution.py:284
  51.8 3.2 %collective-permute-start = (f32[96,128]{1,0:T(8,128)S(1)}, f32[96,128]{1,0:T(8,128)S(1)}, u32[]{:S(2)}, u32[]{:S(2)}) collective-permute-start(f32[96,128]{1,0:T(8,128)S(1)} %get-tuple-element.8), channel_id=1, source_target_pairs={{0,1},{1,0},{2,3},{3,2},{4,5},{5,4},{6,7},{7,6},{8,9},{9,8},{10,11... | collective-permute-start | bytes 147464 | tf_op jit(solution)/shard_map/ppermute | solution.py:241
  55.0 18.3 %collective-permute-start.3 = (f32[96,128]{1,0:T(8,128)S(1)}, f32[96,128]{1,0:T(8,128)S(1)}, u32[]{:S(2)}, u32[]{:S(2)}) collective-permute-start(f32[96,128]{1,0:T(8,128)S(1)} %add.9.own_ref), channel_id=1, source_target_pairs={{0,4},{2,6},{4,8},{6,10},{8,12},{10,14},{12,16},{14,18},{16,20},{1... | collective-permute-start | bytes 147464 | tf_op jit(solution)/shard_map/ppermute | solution.py:237
  61.0 12.8 %collective-permute-start.2 = (f32[96,128]{1,0:T(8,128)S(1)}, f32[96,128]{1,0:T(8,128)S(1)}, u32[]{:S(2)}, u32[]{:S(2)}) collective-permute-start(f32[96,128]{1,0:T(8,128)S(1)} %add.9.own_ref), channel_id=1, source_target_pairs={{0,2},{2,4},{4,6},{6,8},{8,10},{10,12},{12,14},{14,16},{16,18},{18... | collective-permute-start | bytes 147464 | tf_op jit(solution)/shard_map/ppermute | solution.py:237
  65.3 9.8 %collective-permute-start.1 = (f32[96,128]{1,0:T(8,128)S(1)}, f32[96,128]{1,0:T(8,128)S(1)}, u32[]{:S(2)}, u32[]{:S(2)}) collective-permute-start(f32[96,128]{1,0:T(8,128)S(1)} %add.9.own_ref), channel_id=1, source_target_pairs={{0,22},{2,0},{4,2},{6,4},{8,6},{10,8},{12,10},{14,12},{16,14},{18,... | collective-permute-start | bytes 147464 | tf_op jit(solution)/shard_map/ppermute | solution.py:237
  75.1 12.8 %collective-permute-start.5 = (f32[96,128]{1,0:T(8,128)S(1)}, f32[96,128]{1,0:T(8,128)S(1)}, u32[]{:S(2)}, u32[]{:S(2)}) collective-permute-start(f32[96,128]{1,0:T(8,128)S(1)} %shard_map.125.step1_ref), channel_id=1, source_target_pairs={{0,8},{2,10},{4,12},{6,14},{8,16},{10,18},{12,20},{14,22},{16,0},{... | collective-permute-start | bytes 147464 | tf_op jit(solution)/shard_map/ppermute | solution.py:237
  81.9 9.9 %collective-permute-start.4 = (f32[96,128]{1,0:T(8,128)S(1)}, f32[96,128]{1,0:T(8,128)S(1)}, u32[]{:S(2)}, u32[]{:S(2)}) collective-permute-start(f32[96,128]{1,0:T(8,128)S(1)} %shard_map.125.step1_ref), channel_id=1, source_target_pairs={{0,16},{2,18},{4,20},{6,22},{8,0},{10,2},{12,4},{14,6},{16,8},{18,... | collective-permute-start | bytes 147464 | tf_op jit(solution)/shard_map/ppermute | solution.py:237
  86.7 1.2 copy-start
  87.9 3.9 %copy-start.2 = (f32[96,128]{1,0:T(8,128)}, f32[96,128]{1,0:T(8,128)S(1)}, u32[]{:S(2)}) copy-start(f32[96,128]{1,0:T(8,128)S(1)} %collective-permute-done.5.after2_ref.step2_ref) | copy-start | bytes 147460
  91.8 0.6 copy-start.4
  92.4 10.4 %copy-start.3 = (f32[96,128]{1,0:T(8,128)S(1)}, f32[96,128]{1,0:T(8,128)}, u32[]{:S(2)}) copy-start(f32[96,128]{1,0:T(8,128)} %copy-done.2) | copy-start | bytes 147460
  92.4 10.4 %copy-start.5 = (f32[96,128]{1,0:T(8,128)S(1)}, f32[96,128]{1,0:T(8,128)}, u32[]{:S(2)}) copy-start(f32[96,128]{1,0:T(8,128)} %copy-done.4) | copy-start | bytes 147460
  92.4 68.9 %all-to-all-start.2 = ((f32[96,32,128]{2,1,0:T(8,128)}), f32[96,32,128]{2,1,0:T(8,128)S(1)}, u32[]{:S(2)}, u32[]{:S(2)}) async-start(f32[96,32,128]{2,1,0:T(8,128)} %bitcast.1), calls=%async_computation.2 | async-start | bytes 3145728 | tf_op jit(solution)/shard_map/all_to_all | solution.py:323
  102.9 5.6 %collective-permute-start.6 = (f32[16,128]{1,0:T(8,128)S(1)}, f32[16,128]{1,0:T(8,128)S(1)}, u32[]{:S(2)}, u32[]{:S(2)}) collective-permute-start(f32[16,128]{1,0:T(8,128)S(1)} %get-tuple-element.15), channel_id=1, source_target_pairs={{0,24},{24,0},{48,72},{72,48},{96,120},{120,96},{144,168},{168,144... | collective-permute-start | bytes 24584 | tf_op jit(solution)/shard_map/ppermute | solution.py:241
  108.5 7.4 %collective-permute-start.7 = (f32[32,128]{1,0:T(8,128)S(1)}, f32[32,128]{1,0:T(8,128)S(1)}, u32[]{:S(2)}, u32[]{:S(2)}) collective-permute-start(f32[32,128]{1,0:T(8,128)S(1)} %pad_maximum_fusion.2), channel_id=1, source_target_pairs={{0,48},{24,72},{48,0},{72,24},{96,144},{120,168},{144,96},{168,120... | collective-permute-start | bytes 49160 | tf_op jit(solution)/shard_map/ppermute | solution.py:241
  115.9 9.7 %collective-permute-start.8 = (f32[64,128]{1,0:T(8,128)S(1)}, f32[64,128]{1,0:T(8,128)S(1)}, u32[]{:S(2)}, u32[]{:S(2)}) collective-permute-start(f32[64,128]{1,0:T(8,128)S(1)} %pad_maximum_fusion.1), channel_id=1, source_target_pairs={{0,96},{24,120},{48,144},{72,168},{96,0},{120,24},{144,48},{168,72... | collective-permute-start | bytes 98312 | tf_op jit(solution)/shard_map/ppermute | solution.py:241
  125.7 7.9 %collective-permute-start.9 = (f32[128,128]{1,0:T(8,128)S(1)}, f32[128,128]{1,0:T(8,128)S(1)}, u32[]{:S(2)}, u32[]{:S(2)}) collective-permute-start(f32[128,128]{1,0:T(8,128)S(1)} %pad_maximum_fusion), channel_id=1, source_target_pairs={{0,192},{192,0},{384,576},{576,384},{1,193},{193,1},{385,577},{577... | collective-permute-start | bytes 196616 | tf_op jit(solution)/shard_map/ppermute | solution.py:241
  133.6 8.4 %collective-permute-start.10 = (f32[256,128]{1,0:T(8,128)S(1)}, f32[256,128]{1,0:T(8,128)S(1)}, u32[]{:S(2)}, u32[]{:S(2)}) collective-permute-start(f32[256,128]{1,0:T(8,128)S(1)} %get-tuple-element.11), channel_id=1, source_target_pairs={{0,384},{192,576},{384,0},{576,192},{1,385},{193,577},{385,1},{577... | collective-permute-start | bytes 393224 | tf_op jit(solution)/shard_map/ppermute | solution.py:241
  142.0 5.2 %collective-permute-start.11 = (f32[512,128]{1,0:T(8,128)S(1)}, f32[512,128]{1,0:T(8,128)S(1)}, u32[]{:S(2)}, u32[]{:S(2)}) collective-permute-start(f32[512,128]{1,0:T(8,128)S(1)} %constant_dynamic-update-slice_fusion.5.own_ref), channel_id=1, source_target_pairs={{0,1},{1,0},{2,3},{3,2},{4,5},{5,4},{6,7},{7,6},{8,9},{9,8},{10,11... | collective-permute-start | bytes 786440 | tf_op jit(solution)/shard_map/ppermute | solution.py:241
  143.9 3.3 %collective-permute-start.12 = (f32[64,128]{1,0:T(8,128)S(1)}, f32[64,128]{1,0:T(8,128)S(1)}, u32[]{:S(2)}, u32[]{:S(2)}) collective-permute-start(f32[64,128]{1,0:T(8,128)S(1)} %slice.24.own_rem_ref), channel_id=1, source_target_pairs={{0,1},{1,0},{2,3},{3,2},{4,5},{5,4},{6,7},{7,6},{8,9},{9,8},{10,11... | collective-permute-start | bytes 98312 | tf_op jit(solution)/shard_map/ppermute | solution.py:241

commit v3 on v2

--- a/solution.py
+++ b/solution.py
@@ -19,7 +19,7 @@
 DEVICES = GRP * NZ * NC
 HID = 512
 TROWS = HID // GRP
-PIECE = 72
+PIECE = 65
 PLANE = NX * NC
 SHEET = NY * NZ
 CHAIN = 96
@@ -82,36 +82,34 @@
     copies[0].wait()
     copies[1].wait()
     tower = lax.dot_general(tin_ref[...], tcot_ref[...], (((0,), (0,)), ((), ())), preferred_element_type=F32)
-    tower = tower.reshape(GRP, TROWS, E)
-    out_ref[:, 32:48, :] = tower[:, :, :LANES]
-    out_ref[:, 48:64, :] = tower[:, :, LANES:]
-    labels = jnp.broadcast_to(rows_ref[...], (GRP, GRP * RCAP))
-    slot = lax.broadcasted_iota(jnp.int32, (GRP, GRP * RCAP), 1)
-    group = lax.broadcasted_iota(jnp.int32, (GRP, GRP * RCAP), 0)
-    labels = jnp.where(slot // RCAP == group, labels, 0).astype(F32).astype(BF16)
-    slot = lax.broadcasted_iota(jnp.int32, (GRP * RCAP, LANES), 0)
-    lane = lax.broadcasted_iota(jnp.int32, (GRP * RCAP, LANES), 1)
-    spread = jnp.where(slot % RCAP == lane % RCAP, 1.0, 0.0).astype(BF16)
-    labels = jnp.dot(labels, spread, preferred_element_type=F32)
-    count = DEVICES * QCAP
-    slot = lax.broadcasted_iota(jnp.int32, (GRP, count), 1)
-    group = lax.broadcasted_iota(jnp.int32, (GRP, count), 0)
-    onward = jnp.where(slot // (count // GRP) == group, jnp.broadcast_to(qrows_ref[...], (GRP, count)), 0).astype(F32).astype(BF16)
-    slot = lax.broadcasted_iota(jnp.int32, (count, LANES), 0)
-    lane = lax.broadcasted_iota(jnp.int32, (count, LANES), 1)
-    spread = jnp.where(slot % (count // GRP) == lane, 1.0, 0.0).astype(BF16)
-    onward = jnp.dot(onward, spread, preferred_element_type=F32)
-    line = lax.broadcasted_iota(jnp.int32, (GRP, 8, LANES), 1)
-    out_ref[:, 64:72, :] = jnp.where(line == 0, labels[:, None, :], onward[:, None, :])
+    for g in range(GRP):
+        for h in range(2):
+            rows = slice(g * PIECE + 32 + 16 * h, g * PIECE + 48 + 16 * h)
+            out_ref[rows, :] = tower[g * TROWS : (g + 1) * TROWS, h * LANES : (h + 1) * LANES]
+    labels = None
+    for ref, first in ((qrows_ref, 0), (rows_ref, 48)):
+        count = ref.shape[1]
+        each = count // GRP
+        slot = lax.broadcasted_iota(jnp.int32, (GRP, count), 1)
+        group = lax.broadcasted_iota(jnp.int32, (GRP, count), 0)
+        chosen = jnp.where(slot // each == group, jnp.broadcast_to(ref[...], (GRP, count)), 0).astype(F32).astype(BF16)
+        slot = lax.broadcasted_iota(jnp.int32, (count, LANES), 0)
+        lane = lax.broadcasted_iota(jnp.int32, (count, LANES), 1)
+        spread = jnp.where(slot % each + first == lane, 1.0, 0.0).astype(BF16)
+        part = jnp.dot(chosen, spread, preferred_element_type=F32)
+        labels = part if labels is None else labels + part
+    out_ref[pl.ds(64, GRP, stride=PIECE), :] = labels
     copies[2].wait()
     copies[3].wait()
     split_terms(bag_smem, bag_ref, pooled_ref, saved_ref, parts_ref)
     slots = slot_ref[...]
     for half in range(2):
-        found = sums(one_hot(slots, half * 256, 256), parts_ref[...]).reshape(GRP // 2, RCAP, E)
-        groups = pl.ds(half * (GRP // 2), GRP // 2)
-        out_ref[groups, 0:16, :] = found[:, :, :LANES]
-        out_ref[groups, 16:32, :] = found[:, :, LANES:]
+        found = sums(one_hot(slots, half * 256, 256), parts_ref[...])
+        for k in range(GRP // 2):
+            first = (half * (GRP // 2) + k) * PIECE
+            for h in range(2):
+                rows = slice(first + 16 * h, first + 16 * h + 16)
+                out_ref[rows, :] = found[k * RCAP : (k + 1) * RCAP, h * LANES : (h + 1) * LANES]
 
 
 def large_kernel(bag_smem, bag_ref, pooled_ref, saved_ref, slot_ref, out_ref, parts_ref):
@@ -142,19 +140,21 @@
 
 
 def merge_kernel(got_ref, keep_ref, give_ref, onward_ref):
-    source = lax.broadcasted_iota(jnp.int32, (8, 8, LANES), 0)
-    lane = lax.broadcasted_iota(jnp.int32, (8, 8, LANES), 2)
-    labels = []
-    for k in range(GRP // 8):
-        rows = jnp.where(lane // RCAP == source, got_ref[8 * k : 8 * k + 8, 64:72, :], 0.0)
-        labels.append(jnp.sum(rows, axis=0)[0:1, :])
-    pick = one_hot(jnp.concatenate(labels, axis=1).astype(jnp.int32), 0, RROWS)
+    known = got_ref[pl.ds(64, GRP, stride=PIECE), :].astype(BF16)
+    line = lax.broadcasted_iota(jnp.int32, (LANES, GRP * RCAP), 0)
+    slot = lax.broadcasted_iota(jnp.int32, (LANES, GRP * RCAP), 1)
+    labels = jnp.dot(known, jnp.where(line == slot % RCAP + 48, 1.0, 0.0).astype(BF16), preferred_element_type=F32)
+    source = lax.broadcasted_iota(jnp.int32, (GRP, GRP * RCAP), 0)
+    slot = lax.broadcasted_iota(jnp.int32, (GRP, GRP * RCAP), 1)
+    labels = jnp.sum(jnp.where(slot // RCAP == source, labels, 0.0), axis=0, keepdims=True)
+    pick = one_hot(labels.astype(jnp.int32), 0, RROWS)
     core = lax.axis_index("c")
     for h in range(2):
-        values = got_ref[:, 16 * h : 16 * h + 16, :].reshape(GRP * RCAP, LANES)
+        values = [got_ref[g * PIECE + 16 * h : g * PIECE + 16 * h + 16, :] for g in range(GRP)]
+        values = jnp.concatenate(values, axis=0)
         both = jnp.dot(pick, halves(values), preferred_element_type=F32)
         remainder = both[:, :LANES] + both[:, LANES:]
-        tower = jnp.sum(got_ref[:, 32 + 16 * h : 48 + 16 * h, :], axis=0)
+        tower = sum(got_ref[g * PIECE + 32 + 16 * h : g * PIECE + 48 + 16 * h, :] for g in range(GRP))
         for kept, ref in ((True, keep_ref), (False, give_ref)):
 
             @pl.when((core == h) == kept)
@@ -162,8 +162,6 @@
                 ref[0:RROWS, :] = remainder
                 ref[RROWS:SUMS, :] = tower
 
-    line = lax.broadcasted_iota(jnp.int32, (GRP, 8, LANES), 1)
-    known = jnp.sum(jnp.where(line == 1, got_ref[:, 64:72, :], 0.0), axis=1).astype(BF16)
     group = lax.broadcasted_iota(jnp.int32, (GRP, LANES), 0)
     lane = lax.broadcasted_iota(jnp.int32, (GRP, LANES), 1)
     total = None
@@ -256,7 +254,7 @@
     parts = pltpu.VMEM((LOOK, 2 * E), BF16)
     pieces = call(
         small_kernel,
-        jax.ShapeDtypeStruct((GRP, PIECE, LANES), F32),
+        jax.ShapeDtypeStruct((GRP * PIECE, LANES), F32),
         (lookup_bag, lookup_bag, remainder_slot, remainder_rows, quotient_rows, pooled_grad, saved_quotient, tower_inputs, tower_cotangent),
         [SMEM] + [VMEM] * 4 + [ANY] * 4,
         [
@@ -271,6 +269,7 @@
         nbytes=3 * 10**6,
         room=56,
     )
+    pieces = pieces.reshape(GRP, 1, PIECE * LANES)
     got = lax.all_to_all(pieces, ("x", "y"), split_axis=0, concat_axis=0, tiled=True)
     outgoing = call(
         large_kernel,
@@ -287,7 +286,7 @@
     keep, give = call(
         merge_kernel,
         (chain, chain),
-        (got,),
+        (got.reshape(GRP * PIECE, LANES),),
         [VMEM],
         [pltpu.VMEM((LANES, LANES), F32)],
         flops=10**8,

time: 164 us -> 161 us (0.982)
  the two profiles are of different devices: /device:TPU:8 before, /device:TPU:12 now
where the time goes in v3:
time: 161 us; the launch traced here: 160 us
  starting transfers between devices  81.1 us (50%)
  waiting for transfers between devices  60.6 us (38%)
  Pallas kernels  14.3 us (9%)
  local copies, waits for them, and re-layouts  3.04 us (2%)
    ppermute x5, starting transfers between devices, shift(): return lax.ppermute(value, 'z', [(i, (i + by) % NZ) for i in range(NZ)])  28.1 us
    ppermute x8, starting transfers between devices, swap(): lax.ppermute(value, axis, [(i, i ^ bit) for i in range(lax.axis_size(axis...  24.6 us
    ppermute x8, waiting for transfers between devices, swap(): lax.ppermute(value, axis, [(i, i ^ bit) for i in range(lax.axis_size(axis...  22.3 us
    all_to_all x1, waiting for transfers between devices, local(): lax.all_to_all(pieces, ('x', 'y'), split_axis=0, concat_axis=0, tiled=True)  18.7 us
    pallas_call x7, Pallas kernels, call(): pl.pallas_call(body, out_shape=out_shape, in_specs=specs, out_specs=jax.t...  14.3 us
    all_to_all x1, starting transfers between devices, local(): lax.all_to_all(pieces, ('x', 'y'), split_axis=0, concat_axis=0, tiled=True)  13.2 us
    all_to_all x1, waiting for transfers between devices, local(): lax.all_to_all(turned.reshape(SHEET, 32, LANES), ('y', 'z'), split_axis=0...  11.5 us
    all_to_all x1, starting transfers between devices, local(): lax.all_to_all(turned.reshape(SHEET, 32, LANES), ('y', 'z'), split_axis=0...  9.73 us
  transfers between devices with their start and end apart: 16, of which 12 were waited for; matrix products, arithmetic and copies ran while one was open for 0% of the time, Pallas kernels for 5%

profile of v3, /device:TPU:12, one launch (start us, length us, event | category | flops | bytes accessed | tf_op | source)
XLA Modules:
  0.0 160.0 jit_solution(12181606537227102704)
XLA Ops:
  0.6 5.2 %shard_map.123 = f32[2080,128]{1,0:T(8,128)} custom-call(s32[1,2048]{1,0:T(1,128)} %bag_ref.3, s32[1,2048]{1,0:T(1,128)} %bag_ref.3, s32[1,2048]{1,0:T(1,128)} %slot_ref.3, s32[1,512]{1,0:T(1,128)} %rows_ref.1, s32[1,1536]{1,0:T(1,128)} %qrows_ref.1, bf16[1024,256]{1,0:T(8,128)(2,1)} %pooled_hbm.1, bf16[2048,256]{1,0:T(8,128)(2,1)} %saved_hbm.1, ...), custom_call_target="tpu_custom_call" | custom-call | flops 2000000000 | bytes 3000000 | tf_op jit(solution)/shard_map/pallas_call | solution.py:36
  5.8 0.0 copy-start.6
  5.8 0.0 copy-start.7
  5.9 0.0 copy-start.8
  5.9 0.0 copy-start.9
  5.9 13.2 %all-to-all-start.1 = ((f32[32,1,8320]{2,1,0:T(1,128)}), f32[32,1,8320]{2,1,0:T(1,128)S(1)}, u32[]{:S(2)}, u32[]{:S(2)}) async-start(f32[32,1,8320]{2,1,0:T(1,128)} %bitcast.5), calls=%async_computation.1 | async-start | bytes 2129920 | tf_op jit(solution)/shard_map/all_to_all | solution.py:273
  19.1 0.0 copy-done.6
  19.1 0.0 copy-done.7
  19.2 0.0 copy-done.8
  19.2 0.0 copy-done.9
  19.2 4.6 %shard_map.121 = f32[8,384,128]{2,1,0:T(8,128)S(1)} custom-call(s32[1,2048]{1,0:T(1,128)S(1)} %copy-done.8, s32[1,2048]{1,0:T(1,128)S(1)} %copy-done.8, bf16[1024,256]{1,0:T(8,128)(2,1)S(1)} %copy-done.7, bf16[2048,256]{1,0:T(8,128)(2,1)S(1)} %copy-done.6, s32[1,2048]{1,0:T(1,128)S(1)} %copy-done.9), custom_call_target="tpu_custom_call" | custom-call | flops 8000000000 | bytes 5000000 | tf_op jit(solution)/shard_map/pallas_call | solution.py:36
  23.8 0.0 copy-start.1
  23.8 1.2 copy-done.1
  24.9 18.7 %all-to-all-done.1 = f32[32,1,8320]{2,1,0:T(1,128)S(1)} async-done(((f32[32,1,8320]{2,1,0:T(1,128)}), f32[32,1,8320]{2,1,0:T(1,128)S(1)}, u32[]{:S(2)}, u32[]{:S(2)}) %all-to-all-start.1) | async-done | bytes 1064992 | tf_op jit(solution)/shard_map/all_to_all | solution.py:273
  43.7 5.4 %all-to-all-start = ((f32[8,384,128]{2,1,0:T(8,128)}), f32[8,384,128]{2,1,0:T(8,128)S(1)}, u32[]{:S(2)}, u32[]{:S(2)}) async-start(f32[8,384,128]{2,1,0:T(8,128)} %copy-done.1), calls=%async_computation | async-start | bytes 3145728 | tf_op jit(solution)/shard_map/all_to_all | solution.py:283
  49.1 0.7 shard_map.124
  49.9 2.1 %collective-permute-start = (f32[96,128]{1,0:T(8,128)S(1)}, f32[96,128]{1,0:T(8,128)S(1)}, u32[]{:S(2)}, u32[]{:S(2)}) collective-permute-start(f32[96,128]{1,0:T(8,128)S(1)} %get-tuple-element.8), channel_id=1, source_target_pairs={{0,1},{1,0},{2,3},{3,2},{4,5},{5,4},{6,7},{7,6},{8,9},{9,8},{10,11... | collective-permute-start | bytes 147464 | tf_op jit(solution)/shard_map/ppermute | solution.py:239
  51.9 1.1 collective-permute-done
  53.0 14.5 %collective-permute-start.1 = (f32[96,128]{1,0:T(8,128)S(1)}, f32[96,128]{1,0:T(8,128)S(1)}, u32[]{:S(2)}, u32[]{:S(2)}) collective-permute-start(f32[96,128]{1,0:T(8,128)S(1)} %add.9.own_ref), channel_id=1, source_target_pairs={{0,22},{2,0},{4,2},{6,4},{8,6},{10,8},{12,10},{14,12},{16,14},{18,... | collective-permute-start | bytes 147464 | tf_op jit(solution)/shard_map/ppermute | solution.py:235
  67.5 1.9 %collective-permute-start.2 = (f32[96,128]{1,0:T(8,128)S(1)}, f32[96,128]{1,0:T(8,128)S(1)}, u32[]{:S(2)}, u32[]{:S(2)}) collective-permute-start(f32[96,128]{1,0:T(8,128)S(1)} %add.9.own_ref), channel_id=1, source_target_pairs={{0,2},{2,4},{4,6},{6,8},{8,10},{10,12},{12,14},{14,16},{16,18},{18... | collective-permute-start | bytes 147464 | tf_op jit(solution)/shard_map/ppermute | solution.py:235
  69.4 1.9 %collective-permute-start.3 = (f32[96,128]{1,0:T(8,128)S(1)}, f32[96,128]{1,0:T(8,128)S(1)}, u32[]{:S(2)}, u32[]{:S(2)}) collective-permute-start(f32[96,128]{1,0:T(8,128)S(1)} %add.9.own_ref), channel_id=1, source_target_pairs={{0,4},{2,6},{4,8},{6,10},{8,12},{10,14},{12,16},{14,18},{16,20},{1... | collective-permute-start | bytes 147464 | tf_op jit(solution)/shard_map/ppermute | solution.py:235
  71.4 0.0 collective-permute-done.1.up_ref
  71.4 3.3 %collective-permute-done.2.down1_ref = f32[96,128]{1,0:T(8,128)S(1)} collective-permute-done((f32[96,128]{1,0:T(8,128)S(1)}, f32[96,128]{1,0:T(8,128)S(1)}, u32[]{:S(2)}, u32[]{:S(2)}) %collective-permute-start.2) | collective-permute-done | bytes 49184 | tf_op jit(solution)/shard_map/ppermute | solution.py:235
  74.7 3.1 %collective-permute-done.3.down2_ref = f32[96,128]{1,0:T(8,128)S(1)} collective-permute-done((f32[96,128]{1,0:T(8,128)S(1)}, f32[96,128]{1,0:T(8,128)S(1)}, u32[]{:S(2)}, u32[]{:S(2)}) %collective-permute-start.3) | collective-permute-done | bytes 49184 | tf_op jit(solution)/shard_map/ppermute | solution.py:235
  77.8 4.0 %collective-permute-start.4 = (f32[96,128]{1,0:T(8,128)S(1)}, f32[96,128]{1,0:T(8,128)S(1)}, u32[]{:S(2)}, u32[]{:S(2)}) collective-permute-start(f32[96,128]{1,0:T(8,128)S(1)} %shard_map.125.step1_ref), channel_id=1, source_target_pairs={{0,16},{2,18},{4,20},{6,22},{8,0},{10,2},{12,4},{14,6},{16,8},{18,... | collective-permute-start | bytes 147464 | tf_op jit(solution)/shard_map/ppermute | solution.py:235
  81.8 5.8 %collective-permute-start.5 = (f32[96,128]{1,0:T(8,128)S(1)}, f32[96,128]{1,0:T(8,128)S(1)}, u32[]{:S(2)}, u32[]{:S(2)}) collective-permute-start(f32[96,128]{1,0:T(8,128)S(1)} %shard_map.125.step1_ref), channel_id=1, source_target_pairs={{0,8},{2,10},{4,12},{6,14},{8,16},{10,18},{12,20},{14,22},{16,0},{... | collective-permute-start | bytes 147464 | tf_op jit(solution)/shard_map/ppermute | solution.py:235
  87.6 0.0 all-to-all-done.got_ref
  87.6 1.6 %shard_map.122.value_ref = f32[3072,128]{1,0:T(8,128)S(1)} custom-call(f32[8,384,128]{2,1,0:T(8,128)S(1)} %all-to-all-done.got_ref), custom_call_target="tpu_custom_call" | custom-call | flops 10000000 | bytes 4000000 | tf_op jit(solution)/shard_map/pallas_call | solution.py:36
  89.2 0.0 copy-start
  89.2 1.2 copy-done
  90.4 0.0 collective-permute-done.4.after1_ref.step0_ref
  90.4 0.0 copy-start.2
  90.4 1.6 %collective-permute-done.5.after2_ref.step2_ref = f32[96,128]{1,0:T(8,128)S(1)} collective-permute-done((f32[96,128]{1,0:T(8,128)S(1)}, f32[96,128]{1,0:T(8,128)S(1)}, u32[]{:S(2)}, u32[]{:S(2)}) %collective-permute-start.5) | collective-permute-done | bytes 49184 | tf_op jit(solution)/shard_map/ppermute | solution.py:235
  92.0 0.0 copy-done.2
  92.0 0.0 copy-start.4
  92.0 0.6 copy-done.4
  92.7 0.0 copy-start.3
  92.7 0.0 copy-start.5
  92.7 9.7 %all-to-all-start.2 = ((f32[96,32,128]{2,1,0:T(8,128)}), f32[96,32,128]{2,1,0:T(8,128)S(1)}, u32[]{:S(2)}, u32[]{:S(2)}) async-start(f32[96,32,128]{2,1,0:T(8,128)} %bitcast.3), calls=%async_computation.2 | async-start | bytes 3145728 | tf_op jit(solution)/shard_map/all_to_all | solution.py:322
  102.4 0.0 copy-done.3
  102.4 0.0 copy-done.5
  102.4 2.6 %collective-permute-start.6 = (f32[16,128]{1,0:T(8,128)S(1)}, f32[16,128]{1,0:T(8,128)S(1)}, u32[]{:S(2)}, u32[]{:S(2)}) collective-permute-start(f32[16,128]{1,0:T(8,128)S(1)} %get-tuple-element.15), channel_id=1, source_target_pairs={{0,24},{24,0},{48,72},{72,48},{96,120},{120,96},{144,168},{168,144... | collective-permute-start | bytes 24584 | tf_op jit(solution)/shard_map/ppermute | solution.py:239
  105.0 4.3 %collective-permute-done.6 = f32[16,128]{1,0:T(8,128)S(1)} collective-permute-done((f32[16,128]{1,0:T(8,128)S(1)}, f32[16,128]{1,0:T(8,128)S(1)}, u32[]{:S(2)}, u32[]{:S(2)}) %collective-permute-start.6) | collective-permute-done | bytes 8224 | tf_op jit(solution)/shard_map/ppermute | solution.py:239
  109.3 3.9 %collective-permute-start.7 = (f32[32,128]{1,0:T(8,128)S(1)}, f32[32,128]{1,0:T(8,128)S(1)}, u32[]{:S(2)}, u32[]{:S(2)}) collective-permute-start(f32[32,128]{1,0:T(8,128)S(1)} %pad_maximum_fusion.2), channel_id=1, source_target_pairs={{0,48},{24,72},{48,0},{72,24},{96,144},{120,168},{144,96},{168,120... | collective-permute-start | bytes 49160 | tf_op jit(solution)/shard_map/ppermute | solution.py:239
  113.3 3.1 %collective-permute-done.7 = f32[32,128]{1,0:T(8,128)S(1)} collective-permute-done((f32[32,128]{1,0:T(8,128)S(1)}, f32[32,128]{1,0:T(8,128)S(1)}, u32[]{:S(2)}, u32[]{:S(2)}) %collective-permute-start.7) | collective-permute-done | bytes 16416 | tf_op jit(solution)/shard_map/ppermute | solution.py:239
  116.3 6.8 %collective-permute-start.8 = (f32[64,128]{1,0:T(8,128)S(1)}, f32[64,128]{1,0:T(8,128)S(1)}, u32[]{:S(2)}, u32[]{:S(2)}) collective-permute-start(f32[64,128]{1,0:T(8,128)S(1)} %pad_maximum_fusion.1), channel_id=1, source_target_pairs={{0,96},{24,120},{48,144},{72,168},{96,0},{120,24},{144,48},{168,72... | collective-permute-start | bytes 98312 | tf_op jit(solution)/shard_map/ppermute | solution.py:239
  123.2 3.4 %collective-permute-done.8 = f32[64,128]{1,0:T(8,128)S(1)} collective-permute-done((f32[64,128]{1,0:T(8,128)S(1)}, f32[64,128]{1,0:T(8,128)S(1)}, u32[]{:S(2)}, u32[]{:S(2)}) %collective-permute-start.8) | collective-permute-done | bytes 32800 | tf_op jit(solution)/shard_map/ppermute | solution.py:239
  126.6 1.9 %collective-permute-start.9 = (f32[128,128]{1,0:T(8,128)S(1)}, f32[128,128]{1,0:T(8,128)S(1)}, u32[]{:S(2)}, u32[]{:S(2)}) collective-permute-start(f32[128,128]{1,0:T(8,128)S(1)} %pad_maximum_fusion), channel_id=1, source_target_pairs={{0,192},{192,0},{384,576},{576,384},{1,193},{193,1},{385,577},{577... | collective-permute-start | bytes 196616 | tf_op jit(solution)/shard_map/ppermute | solution.py:239
  128.5 4.2 %collective-permute-done.9 = f32[128,128]{1,0:T(8,128)S(1)} collective-permute-done((f32[128,128]{1,0:T(8,128)S(1)}, f32[128,128]{1,0:T(8,128)S(1)}, u32[]{:S(2)}, u32[]{:S(2)}) %collective-permute-start.9) | collective-permute-done | bytes 65568 | tf_op jit(solution)/shard_map/ppermute | solution.py:239
  132.8 3.0 %collective-permute-start.10 = (f32[256,128]{1,0:T(8,128)S(1)}, f32[256,128]{1,0:T(8,128)S(1)}, u32[]{:S(2)}, u32[]{:S(2)}) collective-permute-start(f32[256,128]{1,0:T(8,128)S(1)} %get-tuple-element.11), channel_id=1, source_target_pairs={{0,384},{192,576},{384,0},{576,192},{1,385},{193,577},{385,1},{577... | collective-permute-start | bytes 393224 | tf_op jit(solution)/shard_map/ppermute | solution.py:239
  135.8 5.4 %collective-permute-done.10 = f32[256,128]{1,0:T(8,128)S(1)} collective-permute-done((f32[256,128]{1,0:T(8,128)S(1)}, f32[256,128]{1,0:T(8,128)S(1)}, u32[]{:S(2)}, u32[]{:S(2)}) %collective-permute-start.10) | collective-permute-done | bytes 131104 | tf_op jit(solution)/shard_map/ppermute | solution.py:239
  141.2 1.9 %collective-permute-start.11 = (f32[512,128]{1,0:T(8,128)S(1)}, f32[512,128]{1,0:T(8,128)S(1)}, u32[]{:S(2)}, u32[]{:S(2)}) collective-permute-start(f32[512,128]{1,0:T(8,128)S(1)} %constant_dynamic-update-slice_fusion.5.own_ref), channel_id=1, source_target_pairs={{0,1},{1,0},{2,3},{3,2},{4,5},{5,4},{6,7},{7,6},{8,9},{9,8},{10,11... | collective-permute-start | bytes 786440 | tf_op jit(solution)/shard_map/ppermute | solution.py:239
  143.1 2.4 %collective-permute-start.12 = (f32[64,128]{1,0:T(8,128)S(1)}, f32[64,128]{1,0:T(8,128)S(1)}, u32[]{:S(2)}, u32[]{:S(2)}) collective-permute-start(f32[64,128]{1,0:T(8,128)S(1)} %slice.24.own_rem_ref), channel_id=1, source_target_pairs={{0,1},{1,0},{2,3},{3,2},{4,5},{5,4},{6,7},{7,6},{8,9},{9,8},{10,11... | collective-permute-start | bytes 98312 | tf_op jit(solution)/shard_map/ppermute | solution.py:239
  145.5 0.8 collective-permute-done.12.other_rem_ref
  146.3 0.0 collective-permute-done.11.other_ref
  146.4 0.9 shard_map.128
  147.2 11.5 %all-to-all-done.2.got_ref = f32[96,32,128]{2,1,0:T(8,128)S(1)} async-done(((f32[96,32,128]{2,1,0:T(8,128)}), f32[96,32,128]{2,1,0:T(8,128)S(1)}, u32[]{:S(2)}, u32[]{:S(2)}) %all-to-all-start.2) | async-done | bytes 1572896 | tf_op jit(solution)/shard_map/all_to_all | solution.py:322
  158.7 1.3 shard_map.127
  (14 shorter events, 0.1 us)
Async XLA Ops:
  5.8 13.3 %copy-start.6 = (bf16[2048,256]{1,0:T(8,128)(2,1)S(1)}, bf16[2048,256]{1,0:T(8,128)(2,1)}, u32[]{:S(2)}) copy-start(bf16[2048,256]{1,0:T(8,128)(2,1)} %saved_ref.1) | copy-start | bytes 3145732
  5.8 13.3 %copy-start.7 = (bf16[1024,256]{1,0:T(8,128)(2,1)S(1)}, bf16[1024,256]{1,0:T(8,128)(2,1)}, u32[]{:S(2)}) copy-start(bf16[1024,256]{1,0:T(8,128)(2,1)} %pooled_hbm.1) | copy-start | bytes 1572868
  5.9 13.3 %copy-start.8 = (s32[1,2048]{1,0:T(1,128)S(1)}, s32[1,2048]{1,0:T(1,128)}, u32[]{:S(2)}) copy-start(s32[1,2048]{1,0:T(1,128)} %bag_ref.3) | copy-start | bytes 24580
  5.9 13.3 %copy-start.9 = (s32[1,2048]{1,0:T(1,128)S(1)}, s32[1,2048]{1,0:T(1,128)}, u32[]{:S(2)}) copy-start(s32[1,2048]{1,0:T(1,128)} %slot_ref.2) | copy-start | bytes 24580
  5.9 37.8 %all-to-all-start.1 = ((f32[32,1,8320]{2,1,0:T(1,128)}), f32[32,1,8320]{2,1,0:T(1,128)S(1)}, u32[]{:S(2)}, u32[]{:S(2)}) async-start(f32[32,1,8320]{2,1,0:T(1,128)} %bitcast.5), calls=%async_computation.1 | async-start | bytes 2129920 | tf_op jit(solution)/shard_map/all_to_all | solution.py:273
  23.8 1.2 copy-start.1
  43.7 43.9 %all-to-all-start = ((f32[8,384,128]{2,1,0:T(8,128)}), f32[8,384,128]{2,1,0:T(8,128)S(1)}, u32[]{:S(2)}, u32[]{:S(2)}) async-start(f32[8,384,128]{2,1,0:T(8,128)} %copy-done.1), calls=%async_computation | async-start | bytes 3145728 | tf_op jit(solution)/shard_map/all_to_all | solution.py:283
  49.9 3.1 %collective-permute-start = (f32[96,128]{1,0:T(8,128)S(1)}, f32[96,128]{1,0:T(8,128)S(1)}, u32[]{:S(2)}, u32[]{:S(2)}) collective-permute-start(f32[96,128]{1,0:T(8,128)S(1)} %get-tuple-element.8), channel_id=1, source_target_pairs={{0,1},{1,0},{2,3},{3,2},{4,5},{5,4},{6,7},{7,6},{8,9},{9,8},{10,11... | collective-permute-start | bytes 147464 | tf_op jit(solution)/shard_map/ppermute | solution.py:239
  53.0 18.4 %collective-permute-start.1 = (f32[96,128]{1,0:T(8,128)S(1)}, f32[96,128]{1,0:T(8,128)S(1)}, u32[]{:S(2)}, u32[]{:S(2)}) collective-permute-start(f32[96,128]{1,0:T(8,128)S(1)} %add.9.own_ref), channel_id=1, source_target_pairs={{0,22},{2,0},{4,2},{6,4},{8,6},{10,8},{12,10},{14,12},{16,14},{18,... | collective-permute-start | bytes 147464 | tf_op jit(solution)/shard_map/ppermute | solution.py:235
  67.5 7.2 %collective-permute-start.2 = (f32[96,128]{1,0:T(8,128)S(1)}, f32[96,128]{1,0:T(8,128)S(1)}, u32[]{:S(2)}, u32[]{:S(2)}) collective-permute-start(f32[96,128]{1,0:T(8,128)S(1)} %add.9.own_ref), channel_id=1, source_target_pairs={{0,2},{2,4},{4,6},{6,8},{8,10},{10,12},{12,14},{14,16},{16,18},{18... | collective-permute-start | bytes 147464 | tf_op jit(solution)/shard_map/ppermute | solution.py:235
  69.4 8.4 %collective-permute-start.3 = (f32[96,128]{1,0:T(8,128)S(1)}, f32[96,128]{1,0:T(8,128)S(1)}, u32[]{:S(2)}, u32[]{:S(2)}) collective-permute-start(f32[96,128]{1,0:T(8,128)S(1)} %add.9.own_ref), channel_id=1, source_target_pairs={{0,4},{2,6},{4,8},{6,10},{8,12},{10,14},{12,16},{14,18},{16,20},{1... | collective-permute-start | bytes 147464 | tf_op jit(solution)/shard_map/ppermute | solution.py:235
  77.8 12.6 %collective-permute-start.4 = (f32[96,128]{1,0:T(8,128)S(1)}, f32[96,128]{1,0:T(8,128)S(1)}, u32[]{:S(2)}, u32[]{:S(2)}) collective-permute-start(f32[96,128]{1,0:T(8,128)S(1)} %shard_map.125.step1_ref), channel_id=1, source_target_pairs={{0,16},{2,18},{4,20},{6,22},{8,0},{10,2},{12,4},{14,6},{16,8},{18,... | collective-permute-start | bytes 147464 | tf_op jit(solution)/shard_map/ppermute | solution.py:235
  81.8 10.2 %collective-permute-start.5 = (f32[96,128]{1,0:T(8,128)S(1)}, f32[96,128]{1,0:T(8,128)S(1)}, u32[]{:S(2)}, u32[]{:S(2)}) collective-permute-start(f32[96,128]{1,0:T(8,128)S(1)} %shard_map.125.step1_ref), channel_id=1, source_target_pairs={{0,8},{2,10},{4,12},{6,14},{8,16},{10,18},{12,20},{14,22},{16,0},{... | collective-permute-start | bytes 147464 | tf_op jit(solution)/shard_map/ppermute | solution.py:235
  89.2 1.2 copy-start
  90.4 1.6 %copy-start.2 = (f32[96,128]{1,0:T(8,128)}, f32[96,128]{1,0:T(8,128)S(1)}, u32[]{:S(2)}) copy-start(f32[96,128]{1,0:T(8,128)S(1)} %collective-permute-done.4.after1_ref.step0_ref) | copy-start | bytes 147460
  92.0 0.6 copy-start.4
  92.7 9.7 %copy-start.3 = (f32[96,128]{1,0:T(8,128)S(1)}, f32[96,128]{1,0:T(8,128)}, u32[]{:S(2)}) copy-start(f32[96,128]{1,0:T(8,128)} %copy-done.2) | copy-start | bytes 147460
  92.7 9.8 %copy-start.5 = (f32[96,128]{1,0:T(8,128)S(1)}, f32[96,128]{1,0:T(8,128)}, u32[]{:S(2)}) copy-start(f32[96,128]{1,0:T(8,128)} %copy-done.4) | copy-start | bytes 147460
  92.7 66.1 %all-to-all-start.2 = ((f32[96,32,128]{2,1,0:T(8,128)}), f32[96,32,128]{2,1,0:T(8,128)S(1)}, u32[]{:S(2)}, u32[]{:S(2)}) async-start(f32[96,32,128]{2,1,0:T(8,128)} %bitcast.3), calls=%async_computation.2 | async-start | bytes 3145728 | tf_op jit(solution)/shard_map/all_to_all | solution.py:322
  102.4 6.9 %collective-permute-start.6 = (f32[16,128]{1,0:T(8,128)S(1)}, f32[16,128]{1,0:T(8,128)S(1)}, u32[]{:S(2)}, u32[]{:S(2)}) collective-permute-start(f32[16,128]{1,0:T(8,128)S(1)} %get-tuple-element.15), channel_id=1, source_target_pairs={{0,24},{24,0},{48,72},{72,48},{96,120},{120,96},{144,168},{168,144... | collective-permute-start | bytes 24584 | tf_op jit(solution)/shard_map/ppermute | solution.py:239
  109.3 7.0 %collective-permute-start.7 = (f32[32,128]{1,0:T(8,128)S(1)}, f32[32,128]{1,0:T(8,128)S(1)}, u32[]{:S(2)}, u32[]{:S(2)}) collective-permute-start(f32[32,128]{1,0:T(8,128)S(1)} %pad_maximum_fusion.2), channel_id=1, source_target_pairs={{0,48},{24,72},{48,0},{72,24},{96,144},{120,168},{144,96},{168,120... | collective-permute-start | bytes 49160 | tf_op jit(solution)/shard_map/ppermute | solution.py:239
  116.3 10.3 %collective-permute-start.8 = (f32[64,128]{1,0:T(8,128)S(1)}, f32[64,128]{1,0:T(8,128)S(1)}, u32[]{:S(2)}, u32[]{:S(2)}) collective-permute-start(f32[64,128]{1,0:T(8,128)S(1)} %pad_maximum_fusion.1), channel_id=1, source_target_pairs={{0,96},{24,120},{48,144},{72,168},{96,0},{120,24},{144,48},{168,72... | collective-permute-start | bytes 98312 | tf_op jit(solution)/shard_map/ppermute | solution.py:239
  126.6 6.1 %collective-permute-start.9 = (f32[128,128]{1,0:T(8,128)S(1)}, f32[128,128]{1,0:T(8,128)S(1)}, u32[]{:S(2)}, u32[]{:S(2)}) collective-permute-start(f32[128,128]{1,0:T(8,128)S(1)} %pad_maximum_fusion), channel_id=1, source_target_pairs={{0,192},{192,0},{384,576},{576,384},{1,193},{193,1},{385,577},{577... | collective-permute-start | bytes 196616 | tf_op jit(solution)/shard_map/ppermute | solution.py:239
  132.8 8.4 %collective-permute-start.10 = (f32[256,128]{1,0:T(8,128)S(1)}, f32[256,128]{1,0:T(8,128)S(1)}, u32[]{:S(2)}, u32[]{:S(2)}) collective-permute-start(f32[256,128]{1,0:T(8,128)S(1)} %get-tuple-element.11), channel_id=1, source_target_pairs={{0,384},{192,576},{384,0},{576,192},{1,385},{193,577},{385,1},{577... | collective-permute-start | bytes 393224 | tf_op jit(solution)/shard_map/ppermute | solution.py:239
  141.2 5.2 %collective-permute-start.11 = (f32[512,128]{1,0:T(8,128)S(1)}, f32[512,128]{1,0:T(8,128)S(1)}, u32[]{:S(2)}, u32[]{:S(2)}) collective-permute-start(f32[512,128]{1,0:T(8,128)S(1)} %constant_dynamic-update-slice_fusion.5.own_ref), channel_id=1, source_target_pairs={{0,1},{1,0},{2,3},{3,2},{4,5},{5,4},{6,7},{7,6},{8,9},{9,8},{10,11... | collective-permute-start | bytes 786440 | tf_op jit(solution)/shard_map/ppermute | solution.py:239
  143.1 3.3 %collective-permute-start.12 = (f32[64,128]{1,0:T(8,128)S(1)}, f32[64,128]{1,0:T(8,128)S(1)}, u32[]{:S(2)}, u32[]{:S(2)}) collective-permute-start(f32[64,128]{1,0:T(8,128)S(1)} %slice.24.own_rem_ref), channel_id=1, source_target_pairs={{0,1},{1,0},{2,3},{3,2},{4,5},{5,4},{6,7},{7,6},{8,9},{9,8},{10,11... | collective-permute-start | bytes 98312 | tf_op jit(solution)/shard_map/ppermute | solution.py:239

commit v4 on v3

--- a/solution.py
+++ b/solution.py
@@ -79,13 +79,6 @@
     copies = [pltpu.make_async_copy(src, dst, arrivals.at[k]) for k, (src, dst) in enumerate(pairs)]
     for copy in copies:
         copy.start()
-    copies[0].wait()
-    copies[1].wait()
-    tower = lax.dot_general(tin_ref[...], tcot_ref[...], (((0,), (0,)), ((), ())), preferred_element_type=F32)
-    for g in range(GRP):
-        for h in range(2):
-            rows = slice(g * PIECE + 32 + 16 * h, g * PIECE + 48 + 16 * h)
-            out_ref[rows, :] = tower[g * TROWS : (g + 1) * TROWS, h * LANES : (h + 1) * LANES]
     labels = None
     for ref, first in ((qrows_ref, 0), (rows_ref, 48)):
         count = ref.shape[1]
@@ -99,6 +92,13 @@
         part = jnp.dot(chosen, spread, preferred_element_type=F32)
         labels = part if labels is None else labels + part
     out_ref[pl.ds(64, GRP, stride=PIECE), :] = labels
+    copies[0].wait()
+    copies[1].wait()
+    tower = lax.dot_general(tin_ref[...], tcot_ref[...], (((0,), (0,)), ((), ())), preferred_element_type=F32)
+    for g in range(GRP):
+        for h in range(2):
+            rows = slice(g * PIECE + 32 + 16 * h, g * PIECE + 48 + 16 * h)
+            out_ref[rows, :] = tower[g * TROWS : (g + 1) * TROWS, h * LANES : (h + 1) * LANES]
     copies[2].wait()
     copies[3].wait()
     split_terms(bag_smem, bag_ref, pooled_ref, saved_ref, parts_ref)
@@ -315,7 +315,7 @@
     turned = pl.pallas_call(
         pass_kernel,
         out_shape=jax.ShapeDtypeStruct((SHEET * 32, LANES), F32),
-        in_specs=[ANY] * 3,
+        in_specs=[ANY, VMEM, VMEM],
         out_specs=ANY,
         input_output_aliases={0: 0},
     )(turned, steps[0], steps[2])

time: 161 us -> 162 us (level)
  no operation moved by 1% of the time
where the time goes in v4:
time: 162 us; the launch traced here: 161 us
  starting transfers between devices  81.1 us (50%)
  waiting for transfers between devices  60.6 us (37%)
  Pallas kernels  15.1 us (9%)
  local copies, waits for them, and re-layouts  3.04 us (2%)
    ppermute x5, starting transfers between devices, shift(): return lax.ppermute(value, 'z', [(i, (i + by) % NZ) for i in range(NZ)])  28.1 us
    ppermute x8, starting transfers between devices, swap(): lax.ppermute(value, axis, [(i, i ^ bit) for i in range(lax.axis_size(axis...  24.6 us
    ppermute x8, waiting for transfers between devices, swap(): lax.ppermute(value, axis, [(i, i ^ bit) for i in range(lax.axis_size(axis...  22.3 us
    all_to_all x1, waiting for transfers between devices, local(): lax.all_to_all(pieces, ('x', 'y'), split_axis=0, concat_axis=0, tiled=True)  18.7 us
    pallas_call x7, Pallas kernels, call(): pl.pallas_call(body, out_shape=out_shape, in_specs=specs, out_specs=jax.t...  14.3 us
    all_to_all x1, starting transfers between devices, local(): lax.all_to_all(pieces, ('x', 'y'), split_axis=0, concat_axis=0, tiled=True)  13.2 us
    all_to_all x1, waiting for transfers between devices, local(): lax.all_to_all(turned.reshape(SHEET, 32, LANES), ('y', 'z'), split_axis=0...  11.5 us
    all_to_all x1, starting transfers between devices, local(): lax.all_to_all(turned.reshape(SHEET, 32, LANES), ('y', 'z'), split_axis=0...  9.73 us
  transfers between devices with their start and end apart: 16, of which 12 were waited for; matrix products, arithmetic and copies ran while one was open for 0% of the time, Pallas kernels for 5%

profile of v4, /device:TPU:12, one launch (start us, length us, event | category | flops | bytes accessed | tf_op | source)
XLA Modules:
  0.0 160.8 jit_solution(10029058153475798729)
XLA Ops:
  0.6 5.2 %shard_map.123 = f32[2080,128]{1,0:T(8,128)} custom-call(s32[1,2048]{1,0:T(1,128)} %bag_ref.3, s32[1,2048]{1,0:T(1,128)} %bag_ref.3, s32[1,2048]{1,0:T(1,128)} %slot_ref.3, s32[1,512]{1,0:T(1,128)} %rows_ref.1, s32[1,1536]{1,0:T(1,128)} %qrows_ref.1, bf16[1024,256]{1,0:T(8,128)(2,1)} %pooled_hbm.1, bf16[2048,256]{1,0:T(8,128)(2,1)} %saved_hbm.1, ...), custom_call_target="tpu_custom_call" | custom-call | flops 2000000000 | bytes 3000000 | tf_op jit(solution)/shard_map/pallas_call | solution.py:36
  5.9 0.0 copy-start.6
  5.9 0.0 copy-start.7
  5.9 0.0 copy-start.8
  5.9 0.0 copy-start.9
  5.9 13.2 %all-to-all-start.1 = ((f32[32,1,8320]{2,1,0:T(1,128)}), f32[32,1,8320]{2,1,0:T(1,128)S(1)}, u32[]{:S(2)}, u32[]{:S(2)}) async-start(f32[32,1,8320]{2,1,0:T(1,128)} %bitcast.5), calls=%async_computation.1 | async-start | bytes 2129920 | tf_op jit(solution)/shard_map/all_to_all | solution.py:273
  19.2 0.0 copy-done.6
  19.2 0.0 copy-done.7
  19.2 0.0 copy-done.8
  19.2 0.0 copy-done.9
  19.2 4.6 %shard_map.121 = f32[8,384,128]{2,1,0:T(8,128)S(1)} custom-call(s32[1,2048]{1,0:T(1,128)S(1)} %copy-done.8, s32[1,2048]{1,0:T(1,128)S(1)} %copy-done.8, bf16[1024,256]{1,0:T(8,128)(2,1)S(1)} %copy-done.7, bf16[2048,256]{1,0:T(8,128)(2,1)S(1)} %copy-done.6, s32[1,2048]{1,0:T(1,128)S(1)} %copy-done.9), custom_call_target="tpu_custom_call" | custom-call | flops 8000000000 | bytes 5000000 | tf_op jit(solution)/shard_map/pallas_call | solution.py:36
  23.8 0.0 copy-start.1
  23.8 1.2 copy-done.1
  25.0 18.7 %all-to-all-done.1 = f32[32,1,8320]{2,1,0:T(1,128)S(1)} async-done(((f32[32,1,8320]{2,1,0:T(1,128)}), f32[32,1,8320]{2,1,0:T(1,128)S(1)}, u32[]{:S(2)}, u32[]{:S(2)}) %all-to-all-start.1) | async-done | bytes 1064992 | tf_op jit(solution)/shard_map/all_to_all | solution.py:273
  43.7 5.4 %all-to-all-start = ((f32[8,384,128]{2,1,0:T(8,128)}), f32[8,384,128]{2,1,0:T(8,128)S(1)}, u32[]{:S(2)}, u32[]{:S(2)}) async-start(f32[8,384,128]{2,1,0:T(8,128)} %copy-done.1), calls=%async_computation | async-start | bytes 3145728 | tf_op jit(solution)/shard_map/all_to_all | solution.py:283
  49.1 0.7 shard_map.124
  49.9 2.1 %collective-permute-start = (f32[96,128]{1,0:T(8,128)S(1)}, f32[96,128]{1,0:T(8,128)S(1)}, u32[]{:S(2)}, u32[]{:S(2)}) collective-permute-start(f32[96,128]{1,0:T(8,128)S(1)} %get-tuple-element.8), channel_id=1, source_target_pairs={{0,1},{1,0},{2,3},{3,2},{4,5},{5,4},{6,7},{7,6},{8,9},{9,8},{10,11... | collective-permute-start | bytes 147464 | tf_op jit(solution)/shard_map/ppermute | solution.py:239
  51.9 1.1 collective-permute-done
  53.0 14.5 %collective-permute-start.1 = (f32[96,128]{1,0:T(8,128)S(1)}, f32[96,128]{1,0:T(8,128)S(1)}, u32[]{:S(2)}, u32[]{:S(2)}) collective-permute-start(f32[96,128]{1,0:T(8,128)S(1)} %add.9.own_ref), channel_id=1, source_target_pairs={{0,22},{2,0},{4,2},{6,4},{8,6},{10,8},{12,10},{14,12},{16,14},{18,... | collective-permute-start | bytes 147464 | tf_op jit(solution)/shard_map/ppermute | solution.py:235
  67.5 1.9 %collective-permute-start.2 = (f32[96,128]{1,0:T(8,128)S(1)}, f32[96,128]{1,0:T(8,128)S(1)}, u32[]{:S(2)}, u32[]{:S(2)}) collective-permute-start(f32[96,128]{1,0:T(8,128)S(1)} %add.9.own_ref), channel_id=1, source_target_pairs={{0,2},{2,4},{4,6},{6,8},{8,10},{10,12},{12,14},{14,16},{16,18},{18... | collective-permute-start | bytes 147464 | tf_op jit(solution)/shard_map/ppermute | solution.py:235
  69.5 1.9 %collective-permute-start.3 = (f32[96,128]{1,0:T(8,128)S(1)}, f32[96,128]{1,0:T(8,128)S(1)}, u32[]{:S(2)}, u32[]{:S(2)}) collective-permute-start(f32[96,128]{1,0:T(8,128)S(1)} %add.9.own_ref), channel_id=1, source_target_pairs={{0,4},{2,6},{4,8},{6,10},{8,12},{10,14},{12,16},{14,18},{16,20},{1... | collective-permute-start | bytes 147464 | tf_op jit(solution)/shard_map/ppermute | solution.py:235
  71.4 0.0 collective-permute-done.1.up_ref
  71.4 3.3 %collective-permute-done.2.down1_ref = f32[96,128]{1,0:T(8,128)S(1)} collective-permute-done((f32[96,128]{1,0:T(8,128)S(1)}, f32[96,128]{1,0:T(8,128)S(1)}, u32[]{:S(2)}, u32[]{:S(2)}) %collective-permute-start.2) | collective-permute-done | bytes 49184 | tf_op jit(solution)/shard_map/ppermute | solution.py:235
  74.7 3.1 %collective-permute-done.3.down2_ref = f32[96,128]{1,0:T(8,128)S(1)} collective-permute-done((f32[96,128]{1,0:T(8,128)S(1)}, f32[96,128]{1,0:T(8,128)S(1)}, u32[]{:S(2)}, u32[]{:S(2)}) %collective-permute-start.3) | collective-permute-done | bytes 49184 | tf_op jit(solution)/shard_map/ppermute | solution.py:235
  77.8 4.0 %collective-permute-start.4 = (f32[96,128]{1,0:T(8,128)S(1)}, f32[96,128]{1,0:T(8,128)S(1)}, u32[]{:S(2)}, u32[]{:S(2)}) collective-permute-start(f32[96,128]{1,0:T(8,128)S(1)} %shard_map.125.step1_ref), channel_id=1, source_target_pairs={{0,16},{2,18},{4,20},{6,22},{8,0},{10,2},{12,4},{14,6},{16,8},{18,... | collective-permute-start | bytes 147464 | tf_op jit(solution)/shard_map/ppermute | solution.py:235
  81.8 5.8 %collective-permute-start.5 = (f32[96,128]{1,0:T(8,128)S(1)}, f32[96,128]{1,0:T(8,128)S(1)}, u32[]{:S(2)}, u32[]{:S(2)}) collective-permute-start(f32[96,128]{1,0:T(8,128)S(1)} %shard_map.125.step1_ref), channel_id=1, source_target_pairs={{0,8},{2,10},{4,12},{6,14},{8,16},{10,18},{12,20},{14,22},{16,0},{... | collective-permute-start | bytes 147464 | tf_op jit(solution)/shard_map/ppermute | solution.py:235
  87.6 0.0 all-to-all-done.got_ref
  87.6 1.6 shard_map.122.value_ref
  89.2 0.0 copy-start
  89.2 1.2 copy-done
  90.4 0.0 collective-permute-done.4.after1_ref.step0_ref
  90.4 0.0 copy-start.2
  90.4 1.6 %collective-permute-done.5.after2_ref.step2_ref = f32[96,128]{1,0:T(8,128)S(1)} collective-permute-done((f32[96,128]{1,0:T(8,128)S(1)}, f32[96,128]{1,0:T(8,128)S(1)}, u32[]{:S(2)}, u32[]{:S(2)}) %collective-permute-start.5) | collective-permute-done | bytes 49184 | tf_op jit(solution)/shard_map/ppermute | solution.py:235
  92.0 0.0 copy-done.2
  92.0 0.0 copy-start.4
  92.0 0.6 copy-done.4
  92.7 0.8 shard_map.126
  93.5 0.0 copy-start.3
  93.5 0.0 copy-start.5
  93.5 9.7 %all-to-all-start.2 = ((f32[96,32,128]{2,1,0:T(8,128)}), f32[96,32,128]{2,1,0:T(8,128)S(1)}, u32[]{:S(2)}, u32[]{:S(2)}) async-start(f32[96,32,128]{2,1,0:T(8,128)} %bitcast.3), calls=%async_computation.2 | async-start | bytes 3145728 | tf_op jit(solution)/shard_map/all_to_all | solution.py:322
  103.2 0.0 copy-done.3
  103.2 0.0 copy-done.5
  103.3 2.6 %collective-permute-start.6 = (f32[16,128]{1,0:T(8,128)S(1)}, f32[16,128]{1,0:T(8,128)S(1)}, u32[]{:S(2)}, u32[]{:S(2)}) collective-permute-start(f32[16,128]{1,0:T(8,128)S(1)} %get-tuple-element.15), channel_id=1, source_target_pairs={{0,24},{24,0},{48,72},{72,48},{96,120},{120,96},{144,168},{168,144... | collective-permute-start | bytes 24584 | tf_op jit(solution)/shard_map/ppermute | solution.py:239
  105.9 4.3 %collective-permute-done.6 = f32[16,128]{1,0:T(8,128)S(1)} collective-permute-done((f32[16,128]{1,0:T(8,128)S(1)}, f32[16,128]{1,0:T(8,128)S(1)}, u32[]{:S(2)}, u32[]{:S(2)}) %collective-permute-start.6) | collective-permute-done | bytes 8224 | tf_op jit(solution)/shard_map/ppermute | solution.py:239
  110.1 3.9 %collective-permute-start.7 = (f32[32,128]{1,0:T(8,128)S(1)}, f32[32,128]{1,0:T(8,128)S(1)}, u32[]{:S(2)}, u32[]{:S(2)}) collective-permute-start(f32[32,128]{1,0:T(8,128)S(1)} %pad_maximum_fusion.2), channel_id=1, source_target_pairs={{0,48},{24,72},{48,0},{72,24},{96,144},{120,168},{144,96},{168,120... | collective-permute-start | bytes 49160 | tf_op jit(solution)/shard_map/ppermute | solution.py:239
  114.1 3.1 %collective-permute-done.7 = f32[32,128]{1,0:T(8,128)S(1)} collective-permute-done((f32[32,128]{1,0:T(8,128)S(1)}, f32[32,128]{1,0:T(8,128)S(1)}, u32[]{:S(2)}, u32[]{:S(2)}) %collective-permute-start.7) | collective-permute-done | bytes 16416 | tf_op jit(solution)/shard_map/ppermute | solution.py:239
  117.2 6.8 %collective-permute-start.8 = (f32[64,128]{1,0:T(8,128)S(1)}, f32[64,128]{1,0:T(8,128)S(1)}, u32[]{:S(2)}, u32[]{:S(2)}) collective-permute-start(f32[64,128]{1,0:T(8,128)S(1)} %pad_maximum_fusion.1), channel_id=1, source_target_pairs={{0,96},{24,120},{48,144},{72,168},{96,0},{120,24},{144,48},{168,72... | collective-permute-start | bytes 98312 | tf_op jit(solution)/shard_map/ppermute | solution.py:239
  124.0 3.4 %collective-permute-done.8 = f32[64,128]{1,0:T(8,128)S(1)} collective-permute-done((f32[64,128]{1,0:T(8,128)S(1)}, f32[64,128]{1,0:T(8,128)S(1)}, u32[]{:S(2)}, u32[]{:S(2)}) %collective-permute-start.8) | collective-permute-done | bytes 32800 | tf_op jit(solution)/shard_map/ppermute | solution.py:239
  127.5 1.9 %collective-permute-start.9 = (f32[128,128]{1,0:T(8,128)S(1)}, f32[128,128]{1,0:T(8,128)S(1)}, u32[]{:S(2)}, u32[]{:S(2)}) collective-permute-start(f32[128,128]{1,0:T(8,128)S(1)} %pad_maximum_fusion), channel_id=1, source_target_pairs={{0,192},{192,0},{384,576},{576,384},{1,193},{193,1},{385,577},{577... | collective-permute-start | bytes 196616 | tf_op jit(solution)/shard_map/ppermute | solution.py:239
  129.4 4.2 %collective-permute-done.9 = f32[128,128]{1,0:T(8,128)S(1)} collective-permute-done((f32[128,128]{1,0:T(8,128)S(1)}, f32[128,128]{1,0:T(8,128)S(1)}, u32[]{:S(2)}, u32[]{:S(2)}) %collective-permute-start.9) | collective-permute-done | bytes 65568 | tf_op jit(solution)/shard_map/ppermute | solution.py:239
  133.6 3.0 %collective-permute-start.10 = (f32[256,128]{1,0:T(8,128)S(1)}, f32[256,128]{1,0:T(8,128)S(1)}, u32[]{:S(2)}, u32[]{:S(2)}) collective-permute-start(f32[256,128]{1,0:T(8,128)S(1)} %get-tuple-element.11), channel_id=1, source_target_pairs={{0,384},{192,576},{384,0},{576,192},{1,385},{193,577},{385,1},{577... | collective-permute-start | bytes 393224 | tf_op jit(solution)/shard_map/ppermute | solution.py:239
  136.6 5.4 %collective-permute-done.10 = f32[256,128]{1,0:T(8,128)S(1)} collective-permute-done((f32[256,128]{1,0:T(8,128)S(1)}, f32[256,128]{1,0:T(8,128)S(1)}, u32[]{:S(2)}, u32[]{:S(2)}) %collective-permute-start.10) | collective-permute-done | bytes 131104 | tf_op jit(solution)/shard_map/ppermute | solution.py:239
  142.0 1.9 %collective-permute-start.11 = (f32[512,128]{1,0:T(8,128)S(1)}, f32[512,128]{1,0:T(8,128)S(1)}, u32[]{:S(2)}, u32[]{:S(2)}) collective-permute-start(f32[512,128]{1,0:T(8,128)S(1)} %constant_dynamic-update-slice_fusion.5.own_ref), channel_id=1, source_target_pairs={{0,1},{1,0},{2,3},{3,2},{4,5},{5,4},{6,7},{7,6},{8,9},{9,8},{10,11... | collective-permute-start | bytes 786440 | tf_op jit(solution)/shard_map/ppermute | solution.py:239
  143.9 2.4 %collective-permute-start.12 = (f32[64,128]{1,0:T(8,128)S(1)}, f32[64,128]{1,0:T(8,128)S(1)}, u32[]{:S(2)}, u32[]{:S(2)}) collective-permute-start(f32[64,128]{1,0:T(8,128)S(1)} %slice.24.own_rem_ref), channel_id=1, source_target_pairs={{0,1},{1,0},{2,3},{3,2},{4,5},{5,4},{6,7},{7,6},{8,9},{9,8},{10,11... | collective-permute-start | bytes 98312 | tf_op jit(solution)/shard_map/ppermute | solution.py:239
  146.3 0.8 collective-permute-done.12.other_rem_ref
  147.2 0.0 collective-permute-done.11.other_ref
  147.2 0.9 shard_map.128
  148.1 11.5 %all-to-all-done.2.got_ref = f32[96,32,128]{2,1,0:T(8,128)S(1)} async-done(((f32[96,32,128]{2,1,0:T(8,128)}), f32[96,32,128]{2,1,0:T(8,128)S(1)}, u32[]{:S(2)}, u32[]{:S(2)}) %all-to-all-start.2) | async-done | bytes 1572896 | tf_op jit(solution)/shard_map/all_to_all | solution.py:322
  159.5 1.3 shard_map.127
  (13 shorter events, 0.1 us)
Async XLA Ops:
  5.9 13.3 %copy-start.6 = (bf16[2048,256]{1,0:T(8,128)(2,1)S(1)}, bf16[2048,256]{1,0:T(8,128)(2,1)}, u32[]{:S(2)}) copy-start(bf16[2048,256]{1,0:T(8,128)(2,1)} %saved_ref.1) | copy-start | bytes 3145732
  5.9 13.3 %copy-start.7 = (bf16[1024,256]{1,0:T(8,128)(2,1)S(1)}, bf16[1024,256]{1,0:T(8,128)(2,1)}, u32[]{:S(2)}) copy-start(bf16[1024,256]{1,0:T(8,128)(2,1)} %pooled_hbm.1) | copy-start | bytes 1572868
  5.9 13.3 %copy-start.8 = (s32[1,2048]{1,0:T(1,128)S(1)}, s32[1,2048]{1,0:T(1,128)}, u32[]{:S(2)}) copy-start(s32[1,2048]{1,0:T(1,128)} %bag_ref.3) | copy-start | bytes 24580
  5.9 13.3 %copy-start.9 = (s32[1,2048]{1,0:T(1,128)S(1)}, s32[1,2048]{1,0:T(1,128)}, u32[]{:S(2)}) copy-start(s32[1,2048]{1,0:T(1,128)} %slot_ref.2) | copy-start | bytes 24580
  5.9 37.8 %all-to-all-start.1 = ((f32[32,1,8320]{2,1,0:T(1,128)}), f32[32,1,8320]{2,1,0:T(1,128)S(1)}, u32[]{:S(2)}, u32[]{:S(2)}) async-start(f32[32,1,8320]{2,1,0:T(1,128)} %bitcast.5), calls=%async_computation.1 | async-start | bytes 2129920 | tf_op jit(solution)/shard_map/all_to_all | solution.py:273
  23.8 1.2 copy-start.1
  43.7 43.9 %all-to-all-start = ((f32[8,384,128]{2,1,0:T(8,128)}), f32[8,384,128]{2,1,0:T(8,128)S(1)}, u32[]{:S(2)}, u32[]{:S(2)}) async-start(f32[8,384,128]{2,1,0:T(8,128)} %copy-done.1), calls=%async_computation | async-start | bytes 3145728 | tf_op jit(solution)/shard_map/all_to_all | solution.py:283
  49.9 3.1 %collective-permute-start = (f32[96,128]{1,0:T(8,128)S(1)}, f32[96,128]{1,0:T(8,128)S(1)}, u32[]{:S(2)}, u32[]{:S(2)}) collective-permute-start(f32[96,128]{1,0:T(8,128)S(1)} %get-tuple-element.8), channel_id=1, source_target_pairs={{0,1},{1,0},{2,3},{3,2},{4,5},{5,4},{6,7},{7,6},{8,9},{9,8},{10,11... | collective-permute-start | bytes 147464 | tf_op jit(solution)/shard_map/ppermute | solution.py:239
  53.0 18.4 %collective-permute-start.1 = (f32[96,128]{1,0:T(8,128)S(1)}, f32[96,128]{1,0:T(8,128)S(1)}, u32[]{:S(2)}, u32[]{:S(2)}) collective-permute-start(f32[96,128]{1,0:T(8,128)S(1)} %add.9.own_ref), channel_id=1, source_target_pairs={{0,22},{2,0},{4,2},{6,4},{8,6},{10,8},{12,10},{14,12},{16,14},{18,... | collective-permute-start | bytes 147464 | tf_op jit(solution)/shard_map/ppermute | solution.py:235
  67.5 7.2 %collective-permute-start.2 = (f32[96,128]{1,0:T(8,128)S(1)}, f32[96,128]{1,0:T(8,128)S(1)}, u32[]{:S(2)}, u32[]{:S(2)}) collective-permute-start(f32[96,128]{1,0:T(8,128)S(1)} %add.9.own_ref), channel_id=1, source_target_pairs={{0,2},{2,4},{4,6},{6,8},{8,10},{10,12},{12,14},{14,16},{16,18},{18... | collective-permute-start | bytes 147464 | tf_op jit(solution)/shard_map/ppermute | solution.py:235
  69.5 8.4 %collective-permute-start.3 = (f32[96,128]{1,0:T(8,128)S(1)}, f32[96,128]{1,0:T(8,128)S(1)}, u32[]{:S(2)}, u32[]{:S(2)}) collective-permute-start(f32[96,128]{1,0:T(8,128)S(1)} %add.9.own_ref), channel_id=1, source_target_pairs={{0,4},{2,6},{4,8},{6,10},{8,12},{10,14},{12,16},{14,18},{16,20},{1... | collective-permute-start | bytes 147464 | tf_op jit(solution)/shard_map/ppermute | solution.py:235
  77.8 12.6 %collective-permute-start.4 = (f32[96,128]{1,0:T(8,128)S(1)}, f32[96,128]{1,0:T(8,128)S(1)}, u32[]{:S(2)}, u32[]{:S(2)}) collective-permute-start(f32[96,128]{1,0:T(8,128)S(1)} %shard_map.125.step1_ref), channel_id=1, source_target_pairs={{0,16},{2,18},{4,20},{6,22},{8,0},{10,2},{12,4},{14,6},{16,8},{18,... | collective-permute-start | bytes 147464 | tf_op jit(solution)/shard_map/ppermute | solution.py:235
  81.8 10.2 %collective-permute-start.5 = (f32[96,128]{1,0:T(8,128)S(1)}, f32[96,128]{1,0:T(8,128)S(1)}, u32[]{:S(2)}, u32[]{:S(2)}) collective-permute-start(f32[96,128]{1,0:T(8,128)S(1)} %shard_map.125.step1_ref), channel_id=1, source_target_pairs={{0,8},{2,10},{4,12},{6,14},{8,16},{10,18},{12,20},{14,22},{16,0},{... | collective-permute-start | bytes 147464 | tf_op jit(solution)/shard_map/ppermute | solution.py:235
  89.2 1.2 copy-start
  90.4 1.6 %copy-start.2 = (f32[96,128]{1,0:T(8,128)}, f32[96,128]{1,0:T(8,128)S(1)}, u32[]{:S(2)}) copy-start(f32[96,128]{1,0:T(8,128)S(1)} %collective-permute-done.4.after1_ref.step0_ref) | copy-start | bytes 147460
  92.0 0.6 copy-start.4
  93.5 9.7 %copy-start.3 = (f32[96,128]{1,0:T(8,128)S(1)}, f32[96,128]{1,0:T(8,128)}, u32[]{:S(2)}) copy-start(f32[96,128]{1,0:T(8,128)} %copy-done.2) | copy-start | bytes 147460
  93.5 9.8 %copy-start.5 = (f32[96,128]{1,0:T(8,128)S(1)}, f32[96,128]{1,0:T(8,128)}, u32[]{:S(2)}) copy-start(f32[96,128]{1,0:T(8,128)} %copy-done.4) | copy-start | bytes 147460
  93.5 66.1 %all-to-all-start.2 = ((f32[96,32,128]{2,1,0:T(8,128)}), f32[96,32,128]{2,1,0:T(8,128)S(1)}, u32[]{:S(2)}, u32[]{:S(2)}) async-start(f32[96,32,128]{2,1,0:T(8,128)} %bitcast.3), calls=%async_computation.2 | async-start | bytes 3145728 | tf_op jit(solution)/shard_map/all_to_all | solution.py:322
  103.3 6.9 %collective-permute-start.6 = (f32[16,128]{1,0:T(8,128)S(1)}, f32[16,128]{1,0:T(8,128)S(1)}, u32[]{:S(2)}, u32[]{:S(2)}) collective-permute-start(f32[16,128]{1,0:T(8,128)S(1)} %get-tuple-element.15), channel_id=1, source_target_pairs={{0,24},{24,0},{48,72},{72,48},{96,120},{120,96},{144,168},{168,144... | collective-permute-start | bytes 24584 | tf_op jit(solution)/shard_map/ppermute | solution.py:239
  110.1 7.0 %collective-permute-start.7 = (f32[32,128]{1,0:T(8,128)S(1)}, f32[32,128]{1,0:T(8,128)S(1)}, u32[]{:S(2)}, u32[]{:S(2)}) collective-permute-start(f32[32,128]{1,0:T(8,128)S(1)} %pad_maximum_fusion.2), channel_id=1, source_target_pairs={{0,48},{24,72},{48,0},{72,24},{96,144},{120,168},{144,96},{168,120... | collective-permute-start | bytes 49160 | tf_op jit(solution)/shard_map/ppermute | solution.py:239
  117.2 10.3 %collective-permute-start.8 = (f32[64,128]{1,0:T(8,128)S(1)}, f32[64,128]{1,0:T(8,128)S(1)}, u32[]{:S(2)}, u32[]{:S(2)}) collective-permute-start(f32[64,128]{1,0:T(8,128)S(1)} %pad_maximum_fusion.1), channel_id=1, source_target_pairs={{0,96},{24,120},{48,144},{72,168},{96,0},{120,24},{144,48},{168,72... | collective-permute-start | bytes 98312 | tf_op jit(solution)/shard_map/ppermute | solution.py:239
  127.5 6.1 %collective-permute-start.9 = (f32[128,128]{1,0:T(8,128)S(1)}, f32[128,128]{1,0:T(8,128)S(1)}, u32[]{:S(2)}, u32[]{:S(2)}) collective-permute-start(f32[128,128]{1,0:T(8,128)S(1)} %pad_maximum_fusion), channel_id=1, source_target_pairs={{0,192},{192,0},{384,576},{576,384},{1,193},{193,1},{385,577},{577... | collective-permute-start | bytes 196616 | tf_op jit(solution)/shard_map/ppermute | solution.py:239
  133.6 8.4 %collective-permute-start.10 = (f32[256,128]{1,0:T(8,128)S(1)}, f32[256,128]{1,0:T(8,128)S(1)}, u32[]{:S(2)}, u32[]{:S(2)}) collective-permute-start(f32[256,128]{1,0:T(8,128)S(1)} %get-tuple-element.11), channel_id=1, source_target_pairs={{0,384},{192,576},{384,0},{576,192},{1,385},{193,577},{385,1},{577... | collective-permute-start | bytes 393224 | tf_op jit(solution)/shard_map/ppermute | solution.py:239
  142.0 5.2 %collective-permute-start.11 = (f32[512,128]{1,0:T(8,128)S(1)}, f32[512,128]{1,0:T(8,128)S(1)}, u32[]{:S(2)}, u32[]{:S(2)}) collective-permute-start(f32[512,128]{1,0:T(8,128)S(1)} %constant_dynamic-update-slice_fusion.5.own_ref), channel_id=1, source_target_pairs={{0,1},{1,0},{2,3},{3,2},{4,5},{5,4},{6,7},{7,6},{8,9},{9,8},{10,11... | collective-permute-start | bytes 786440 | tf_op jit(solution)/shard_map/ppermute | solution.py:239
  143.9 3.3 %collective-permute-start.12 = (f32[64,128]{1,0:T(8,128)S(1)}, f32[64,128]{1,0:T(8,128)S(1)}, u32[]{:S(2)}, u32[]{:S(2)}) collective-permute-start(f32[64,128]{1,0:T(8,128)S(1)} %slice.24.own_rem_ref), channel_id=1, source_target_pairs={{0,1},{1,0},{2,3},{3,2},{4,5},{5,4},{6,7},{7,6},{8,9},{9,8},{10,11... | collective-permute-start | bytes 98312 | tf_op jit(solution)/shard_map/ppermute | solution.py:239
